TPU v7x, 32 devices: a whole 2x2x4 slice. The times are simulated.
32 devices in a mesh: batch: 2 (over x), head: 2 (over y), blk: 8 (over z, core).
Axes of the slice: x: 2, y: 2, z: 4, core: 2. Of those that a mesh axis runs over, the one named last changes fastest.
Arguments:
- tokens: bfloat16 [16, 2048, 1024], P(('batch', 'blk'), 'head'), parts along dimension 0, may hold values from -10.5 to 10.5
- proj_weight: bfloat16 [1024, 3072], replicated, may hold values from -0.1875 to 0.1875
- out_weight: bfloat16 [1024, 1024], replicated, may hold values from -1.5 to 1.5
- pattern: int32 [256, 16], P(('batch', 'blk')), parts along dimension 0, may hold values from 0 to 127, as said below
Outputs:
- mixed_out: bfloat16 [16, 2048, 1024], P(('batch', 'blk'), 'head'), parts along dimension 0
There are 2 independent parts, one for each index of `batch`. A program takes and returns all parts, laid end to end along the dimension named above; an argument that names none is the same for every part. Nothing has to cross between parts.
Inputs may be any that keep to these rules, and one draw needn't show every extreme that they name: `pattern`: row i lists first 6 distinct blocks j with |j - i| <= 8, among them i itself, then 10 distinct summary blocks j (j % 16 >= 12) with |j - i| > 8. Every row with 8 <= i < 120 lists i - 8 and i + 8.
All inputs are finite; a program needn't handle non-finite values.
Results may differ from a plain program's by a relative error of at most 0.0095.
Values may be sent and summed in bfloat16 or wider, within the bound.
No kernel may reach another device: no remote copies, remote signals or barrier semaphores. Data moves between devices by JAX's collectives and lax.ppermute only.
A program may use at most 128 MiB of HBM per device.

v0:
```python
import functools

import jax
import jax.numpy as jnp
from jax import lax
from jax.experimental import pallas as pl
from jax.experimental.pallas import tpu as pltpu
from jax.sharding import PartitionSpec as P

D = 1024
H = 16
HD = 64
BLK = 128
REACH = 8
LSEL = 6
SUMB = 4
SB = 16
KSEL = 16
PAIRS = H // 2
LANES = 2 * HD
TOTAL_CAP = 2.0**100


def split_kernel(weight_ref, query_ref, key_ref, value_ref):
    both = weight_ref[...]
    first, second = both[:, : 3 * HD], both[:, 3 * HD :]

    def columns(which):
        lo = which * HD
        return jnp.concatenate([first[:, lo : lo + HD], second[:, lo : lo + HD]], axis=1)

    query_ref[...] = columns(0).T
    key_ref[...] = columns(1)
    value_ref[...] = columns(2).T


def split_weights(proj_weight):
    wide = jax.ShapeDtypeStruct((D, D), jnp.bfloat16)
    across = pl.BlockSpec((LANES, D), lambda p: (p, 0))
    down = pl.BlockSpec((D, LANES), lambda p: (0, p))
    return pl.pallas_call(
        split_kernel,
        grid=(PAIRS,),
        in_specs=[pl.BlockSpec((D, 3 * LANES), lambda p: (0, p))],
        out_specs=[across, down, across],
        out_shape=[wide, wide, wide],
        cost_estimate=pl.CostEstimate(flops=0, bytes_accessed=4 * D * 3 * D, transcendentals=0),
        name="split_weights",
    )(proj_weight)


def attend_kernel(blocks, count, chunk, together, pieces, table_ref, query_ref, *refs):
    f32, bf16 = jnp.float32, jnp.bfloat16
    key_pieces, value_pieces = refs[:pieces], refs[pieces : 2 * pieces]
    out_ref, key_ref, value_ref, shift_ref, arrived = refs[2 * pieces :]
    step, steps = pl.program_id(0), pl.num_programs(0)
    slot = lax.rem(step, 2)

    def copies(pair, slot):
        lanes = pl.ds(pl.multiple_of(pair * LANES, LANES), LANES)
        found, start = [], 0
        for n, (key_piece, value_piece) in enumerate(zip(key_pieces, value_pieces)):
            span = pl.ds(start, key_piece.shape[0])
            found += [
                pltpu.make_async_copy(key_piece.at[:, lanes], key_ref.at[slot, span, :], arrived.at[slot, 2 * n]),
                pltpu.make_async_copy(
                    value_piece.at[lanes, :], value_ref.at[slot, :, span], arrived.at[slot, 2 * n + 1]
                ),
            ]
            start += key_piece.shape[0]
        return found

    @pl.when(step == 0)
    def _():
        for copy in copies(0, 0):
            copy.start()

    @pl.when(step + 1 < steps)
    def _():
        for copy in copies(step + 1, 1 - slot):
            copy.start()

    for copy in copies(step, slot):
        copy.wait()

    row = lax.broadcasted_iota(jnp.int32, (LANES, BLK), 0)

    def at(index):
        return pl.ds(pl.multiple_of(index * BLK, BLK), BLK)

    def queries(index):
        own = query_ref[:, at(index)]
        zero = jnp.zeros_like(own)
        return jnp.concatenate([jnp.where(row < HD, own, zero), jnp.where(row < HD, zero, own)], axis=1)

    def places(index, which, size):
        return [at(table_ref[index, which + n]) for n in range(size)]

    def score(index, which, size, query):
        keys = [key_ref[slot, place, :] for place in places(index, which, size)]
        return jnp.dot(jnp.concatenate(keys, axis=0), query, preferred_element_type=f32)

    def gather(index, which, size, raised):
        picked = jnp.concatenate([value_ref[slot, :, place] for place in places(index, which, size)], axis=1)
        ones = jnp.ones((16, raised.shape[0]), bf16)
        return jnp.dot(jnp.concatenate([picked, ones], axis=0), raised, preferred_element_type=f32)

    def finish(index, total):
        count_all = total[LANES : LANES + 1]
        scale = 1.0 / count_all
        mine = jnp.concatenate([total[:HD, :BLK] * scale[:, :BLK], total[HD:LANES, BLK:] * scale[:, BLK:]], axis=0)
        out_ref[at(index), :] = mine.T.astype(bf16)
        return count_all

    for index in range(blocks):
        shift_ref[index : index + 1, :] = jnp.max(score(index, 0, 1, queries(index)), axis=0, keepdims=True)

    def one(index):
        query = queries(index)
        total = None
        shift = shift_ref[pl.ds(index, 1), :]
        for which in range(0, count, chunk):
            raised = jnp.exp(score(index, which, chunk, query) - shift).astype(bf16)
            part = gather(index, which, chunk, raised)
            total = part if total is None else total + part
        return finish(index, total)

    def body(number, peak):
        for n in range(together):
            peak = jnp.maximum(peak, one(number * together + n))
        return peak

    peak = lax.fori_loop(0, blocks // together, body, jnp.zeros((1, 2 * BLK), f32))

    @pl.when(jnp.logical_not(jnp.max(peak) <= TOTAL_CAP))
    def _():
        def whole_row(index, carry):
            query = queries(index)

            def largest(n, shift):
                return jnp.maximum(shift, jnp.max(score(index, 2 * n, 2, query), axis=0, keepdims=True))

            shift = lax.fori_loop(0, count // 2, largest, jnp.full((1, 2 * BLK), -jnp.inf, f32))

            def add(n, total):
                raised = jnp.exp(score(index, 2 * n, 2, query) - shift).astype(bf16)
                return total + gather(index, 2 * n, 2, raised)

            finish(index, lax.fori_loop(0, count // 2, add, jnp.zeros((LANES + 16, 2 * BLK), f32)))
            return carry

        lax.fori_loop(0, blocks, whole_row, 0)


def attend(table, query, keys, values, chunk, together):
    rows = query.shape[1]
    blocks = rows // BLK
    count = table.shape[1]
    while blocks % together:
        together //= 2
    total_rows = sum(key.shape[0] for key in keys)
    scores = rows * count * BLK * H
    scratch = 8 * total_rows * LANES
    return pl.pallas_call(
        functools.partial(attend_kernel, blocks, count, chunk, together, len(keys)),
        grid=(PAIRS,),
        in_specs=[pl.BlockSpec(memory_space=pltpu.SMEM), pl.BlockSpec((LANES, rows), lambda p: (p, 0))]
        + [pl.BlockSpec(memory_space=pl.ANY)] * (2 * len(keys)),
        out_specs=pl.BlockSpec((rows, LANES), lambda p: (0, p)),
        out_shape=jax.ShapeDtypeStruct((rows, D), jnp.bfloat16),
        scratch_shapes=[
            pltpu.VMEM((2, total_rows, LANES), jnp.bfloat16),
            pltpu.VMEM((2, LANES, total_rows), jnp.bfloat16),
            pltpu.VMEM((blocks, 2 * BLK), jnp.float32),
            pltpu.SemaphoreType.DMA((2, 2 * len(keys))),
        ],
        compiler_params=pltpu.CompilerParams(vmem_limit_bytes=scratch + 10 * 2**20),
        cost_estimate=pl.CostEstimate(
            flops=24 * scores * HD, bytes_accessed=4 * total_rows * D + 4 * rows * D, transcendentals=scores
        ),
        name="attend",
    )(table, query, *keys, *values)


def project_rows(rows, weight):
    return jnp.dot(rows, weight, preferred_element_type=jnp.float32).astype(jnp.bfloat16)


def project_columns(weight, rows, scale=1.0):
    wide = lax.dot_general(weight, rows, (((1,), (1,)), ((), ())), preferred_element_type=jnp.float32)
    return (wide * scale).astype(jnp.bfloat16)


def rows_by_axes(own, weights, place, stride, strides):
    summary = SUMB * BLK
    half = summary // 2
    cut = own.shape[0] - summary
    chips = strides // 2
    low = place == 0
    swap = lambda rows: lax.ppermute(rows, "head", [(0, 1), (1, 0)])
    beside = lambda rows: lax.ppermute(rows, "blk", [(s, s ^ 1) for s in range(strides)])

    def along(rows, k):
        return lax.ppermute(rows, "blk", [(s, (s + 2 * k) % strides) for s in range(strides)])

    steps = []
    for s in range(strides - 1):
        steps += [(s, s + 1), (strides + s + 1, strides + s)]
    to_next = lambda rows: lax.ppermute(rows, ("head", "blk"), steps)

    other_end = swap(own[-half:])
    other_end, own, weights = lax.optimization_barrier((other_end, own, weights))
    carried = jnp.where(low, other_end, own[cut : cut + half])
    other = swap(own[:-half])
    edge_end = to_next(other_end)
    ends = [along(carried, 1), along(carried, chips - 1)]
    ends, after = lax.optimization_barrier((jnp.concatenate(ends, axis=0), carried))
    middle = jnp.concatenate([along(after, k) for k in range(2, chips - 1)], axis=0)
    own, other, other_end, released = lax.optimization_barrier((own, other, other_end, ends))
    across_ends = swap(released)
    edge = to_next(other)
    query = project_columns(weights[0], own, HD**-0.5)
    across_ends, middle = lax.optimization_barrier((across_ends, middle))
    across_middle, edge = lax.optimization_barrier((swap(middle), edge))
    nearby = jnp.where(low, jnp.concatenate([other_end, other[-half:]], axis=0), own[cut:])
    pieces = [own, other, other_end, edge, edge_end, beside(nearby)]
    pieces += [ends, middle, beside(ends), beside(middle)]
    pieces += [across_ends, across_middle, beside(across_ends), beside(across_middle)]
    span = 2 * (chips - 1)

    def position(block):
        of, inside = block // SB, block % SB
        rel = block - stride * SB
        mine = inside % 8 + jnp.where(inside // 8 == place, 0, 8)
        edge = jnp.where(rel < 0, rel + SB + 8, rel)
        order = inside - (SB - SUMB)
        k = (stride // 2 - of // 2) % chips
        turn = jnp.where(k == chips - 1, 1, jnp.where(k == 1, 0, k))
        turned = (order // 2 ^ (1 - place)) * 2 + order % 2
        part = jnp.where(of % 2 == stride % 2, 0, 1) + jnp.where(order // 2 == 1 - place, 0, 2)
        far = jnp.where(k == 0, 24 + turned, 28 + part * span + turn * 2 + order % 2)
        return jnp.where(of == stride, mine, edge), jnp.where(of == stride, mine, far)

    return pieces, weights, query, position


def rows_by_gather(own, place, stride, strides, heads):
    summary = SUMB * BLK
    share = summary // heads
    lower = place < heads // 2
    stride_rows = lax.all_gather(own, "head", axis=0, tiled=True)
    piece = lax.dynamic_slice_in_dim(stride_rows[-summary:], place * share, share, 0)
    far_rows = lax.all_gather(piece, ("blk", "head"), axis=0, tiled=True)
    half = stride_rows.shape[0] // 2
    steps = []
    for h in range(heads):
        for s in range(strides - 1):
            ends = (h * strides + s, h * strides + s + 1)
            steps.append(ends if h < heads // 2 else ends[::-1])
    edge = lax.ppermute(jnp.where(lower, stride_rows[half:], stride_rows[:half]), ("head", "blk"), steps)

    def position(block):
        rel = block - stride * SB
        near = jnp.where(rel < 0, rel + SB + REACH, rel)
        return near, SB + REACH + block // SB * SUMB + block % SB - (SB - SUMB)

    return [stride_rows, edge, far_rows], position


def on_device(tokens, proj_weight, out_weight, pattern):
    heads = lax.axis_size("head")
    strides = lax.axis_size("blk")
    place = lax.axis_index("head")
    stride = lax.axis_index("blk")
    own = tokens[0]
    blocks = own.shape[0] // BLK
    weights = split_weights(proj_weight)

    if heads == 2:
        pieces, weights, query, position = rows_by_axes(own, weights, place, stride, strides)
    else:
        pieces, position = rows_by_gather(own, place, stride, strides, heads)
        query = project_columns(weights[0], own, HD**-0.5)
    listed = lax.dynamic_slice_in_dim(pattern, place * blocks, blocks, 0)
    near, far = position(listed)
    table = jnp.where(lax.broadcasted_iota(jnp.int32, listed.shape, 1) < LSEL, near, far)

    _, key_weight, value_weight = weights
    keys = [project_rows(rows, key_weight) for rows in pieces]
    values = [project_columns(value_weight, rows) for rows in pieces]
    mixed = attend(table, query, keys, values, 4, 2)
    out = jnp.dot(mixed, out_weight, preferred_element_type=jnp.float32).astype(jnp.bfloat16)
    return out.reshape(tokens.shape)


def solution(mesh):
    return jax.shard_map(
        on_device,
        mesh=mesh,
        in_specs=(P(("batch", "blk"), "head", None), P(), P(), P(("batch", "blk"), None)),
        out_specs=P(("batch", "blk"), "head", None),
        check_vma=False,
    )
```

profile of v0, /device:TPU:11, one launch (start us, length us, event | category | flops | bytes accessed | tf_op | source)
XLA Modules:
  0.0 467.7 jit_solution(17447791755935765245)
XLA Ops:
  1.2 1.3 collective-permute-start
  2.5 8.6 %split_weights.1 = (bf16[1024,1024]{1,0:T(8,128)(2,1)}, bf16[1024,1024]{1,0:T(8,128)(2,1)}, bf16[1024,1024]{1,0:T(8,128)(2,1)}) custom-call(bf16[1024,3072]{1,0:T(8,128)(2,1)} %weight_ref.1), custom_call_target="tpu_custom_call" | custom-call | bytes 12582912 | tf_op jit(solution)/shard_map/split_weights/pallas_call | solution.py:41
  11.1 3.0 collective-permute-done
  15.4 1.3 collective-permute-start.2
  16.7 5.2 %collective-permute-start.8 = (bf16[256,1024]{1,0:T(8,128)(2,1)S(1)}, bf16[256,1024]{1,0:T(8,128)(2,1)}, u32[]{:S(2)}, u32[]{:S(2)}) collective-permute-start(bf16[256,1024]{1,0:T(8,128)(2,1)S(1)} %collective-permute-done), channel_id=1, source_target_pairs={{0,1},{9,8},{1,2},{10,9},{2,3},{11,10},{3,4},{12,11},{4,5},{13,12}... | collective-permute-start | bytes 1572872 | tf_op jit(solution)/shard_map/ppermute | solution.py:209
  22.0 1.7 slice.20
  23.8 3.4 collective-permute-done.3
  27.2 13.3 %collective-permute-done.2 = bf16[256,1024]{1,0:T(8,128)(2,1)} collective-permute-done((bf16[256,1024]{1,0:T(8,128)(2,1)S(1)}, bf16[256,1024]{1,0:T(8,128)(2,1)}, u32[]{:S(2)}, u32[]{:S(2)}) %collective-permute-start.2) | collective-permute-done | bytes 524320 | tf_op jit(solution)/shard_map/ppermute | solution.py:204
  40.6 1.3 pad_maximum_fusion
  42.5 4.4 collective-permute-start.10
  46.9 1.8 convolution_convert_fusion.20.refs_18_
  48.7 1.8 convolution_convert_fusion.26.refs_4_
  50.5 1.3 convolution_convert_fusion.9.refs_20_
  53.0 6.1 %collective-permute-done.1 = bf16[768,1024]{1,0:T(8,128)(2,1)S(1)} collective-permute-done((bf16[768,1024]{1,0:T(8,128)(2,1)S(1)}, bf16[768,1024]{1,0:T(8,128)(2,1)S(1)}, u32[]{:S(2)}, u32[]{:S(2)}) %collective-permute-start.1) | collective-permute-done | bytes 1572896 | tf_op jit(solution)/shard_map/ppermute | solution.py:200
  59.1 2.3 convolution_convert_fusion.1.refs_0_
  61.5 2.4 convolution_convert_fusion.refs_14_
  64.4 7.4 %collective-permute-start.4 = (bf16[512,1024]{1,0:T(8,128)(2,1)S(1)}, bf16[512,1024]{1,0:T(8,128)(2,1)S(1)}, u32[]{:S(2)}, u32[]{:S(2)}) collective-permute-start(bf16[512,1024]{1,0:T(8,128)(2,1)S(1)} %pad_maximum_fusion), channel_id=1, source_target_pairs={{0,8},{8,0},{1,9},{9,1},{2,10},{10,2},{3,11},{11,3},{4,12},{12,4},... | collective-permute-start | bytes 3145736 | tf_op jit(solution)/shard_map/ppermute | solution.py:200
  71.9 1.8 convolution_convert_fusion.3.refs_15_
  73.7 2.4 multiply_convert_fusion.query_ref
  76.1 1.5 convolution_convert_fusion.8.refs_22_
  78.9 1.8 convolution_convert_fusion.5.refs_1_
  81.4 1.9 collective-permute-start.7
  84.1 10.9 %collective-permute-done.4 = bf16[512,1024]{1,0:T(8,128)(2,1)S(1)} collective-permute-done((bf16[512,1024]{1,0:T(8,128)(2,1)S(1)}, bf16[512,1024]{1,0:T(8,128)(2,1)S(1)}, u32[]{:S(2)}, u32[]{:S(2)}) %collective-permute-start.4) | collective-permute-done | bytes 1048608 | tf_op jit(solution)/shard_map/ppermute | solution.py:200
  96.0 1.5 collective-permute-start.6
  97.7 1.3 convolution_convert_fusion.7.refs_24_
  100.3 1.3 convolution_convert_fusion.10.refs_19_
  105.8 3.7 collective-permute-done.6
  111.9 1.8 convolution_convert_fusion.2.refs_17_
  113.7 1.8 convolution_convert_fusion.4.refs_3_
  115.5 1.5 convolution_convert_fusion.6.refs_26_
  119.8 344.2 %attend.1 = bf16[1024,1024]{1,0:T(8,128)(2,1)S(1)} custom-call(s32[8,16]{1,0:T(8,128)S(1)} %fusion.6.table_ref, bf16[1024,1024]{1,0:T(8,128)(2,1)S(1)} %multiply_convert_fusion.query_ref, bf16[1024,1024]{1,0:T(8,128)(2,1)S(1)} %convolution_convert_fusion.1.refs_0_, bf16[768,1024]{1,0:T(8,128)(2,1)S(1)} %convolution_convert_fusion.5.refs_1_, ...), custom_call_target="tpu_custom_call" | custom-call | flops 51539607552 | bytes 31457280 | tf_op jit(solution)/shard_map/attend/pallas_call | solution.py:164
  464.0 3.7 convert_bitcast_fusion
  (48 shorter events, 19.7 us)
Async XLA Ops:
  0.0 464.0 %copy-start = (bf16[1024,1024]{1,0:T(8,128)(2,1)S(1)}, bf16[1024,1024]{1,0:T(8,128)(2,1)}, u32[]{:S(2)}) copy-start(bf16[1024,1024]{1,0:T(8,128)(2,1)} %param.6) | copy-start | bytes 6291460
  1.2 12.9 %collective-permute-start = (bf16[256,1024]{1,0:T(8,128)(2,1)S(1)}, bf16[256,1024]{1,0:T(8,128)(2,1)S(1)}, u32[]{:S(2)}, u32[]{:S(2)}) collective-permute-start(bf16[256,1024]{1,0:T(8,128)(2,1)S(1)} %slice_bitcast_fusion), channel_id=1, source_target_pairs={{0,8},{8,0},{1,9},{9,1},{2,10},{10,2},{3,11},{11,3},{4,12},{12,4},... | collective-permute-start | bytes 1572872 | tf_op jit(solution)/shard_map/ppermute | solution.py:200
  14.1 9.7 %copy-start.2 = (s32[16,16]{1,0:T(8,128)S(1)}, s32[16,16]{1,0:T(8,128)}, u32[]{:S(2)}) copy-start(s32[16,16]{1,0:T(8,128)} %param.7) | copy-start | bytes 3076
  15.2 12.0 %collective-permute-start.3 = (bf16[256,1024]{1,0:T(8,128)(2,1)S(1)}, bf16[256,1024]{1,0:T(8,128)(2,1)}, u32[]{:S(2)}, u32[]{:S(2)}) collective-permute-start(bf16[256,1024]{1,0:T(8,128)(2,1)S(1)} %slice_select_fusion), channel_id=1, source_target_pairs={{0,6},{1,7},{2,0},{3,1},{4,2},{5,3},{6,4},{7,5},{8,14},{9,15},{10,... | collective-permute-start | bytes 1572872 | tf_op jit(solution)/shard_map/ppermute | solution.py:204
  15.4 25.2 %collective-permute-start.2 = (bf16[256,1024]{1,0:T(8,128)(2,1)S(1)}, bf16[256,1024]{1,0:T(8,128)(2,1)}, u32[]{:S(2)}, u32[]{:S(2)}) collective-permute-start(bf16[256,1024]{1,0:T(8,128)(2,1)S(1)} %slice_select_fusion), channel_id=1, source_target_pairs={{0,2},{1,3},{2,4},{3,5},{4,6},{5,7},{6,0},{7,1},{8,10},{9,11},{10,... | collective-permute-start | bytes 1572872 | tf_op jit(solution)/shard_map/ppermute | solution.py:204
  16.7 30.2 %collective-permute-start.8 = (bf16[256,1024]{1,0:T(8,128)(2,1)S(1)}, bf16[256,1024]{1,0:T(8,128)(2,1)}, u32[]{:S(2)}, u32[]{:S(2)}) collective-permute-start(bf16[256,1024]{1,0:T(8,128)(2,1)S(1)} %collective-permute-done), channel_id=1, source_target_pairs={{0,1},{9,8},{1,2},{10,9},{2,3},{11,10},{3,4},{12,11},{4,5},{13,12}... | collective-permute-start | bytes 1572872 | tf_op jit(solution)/shard_map/ppermute | solution.py:209
  21.9 24.9 %copy-start.4 = (bf16[1024,1024]{1,0:T(8,128)(2,1)S(1)}, bf16[1024,1024]{1,0:T(8,128)(2,1)}, u32[]{:S(2)}) copy-start(bf16[1024,1024]{1,0:T(8,128)(2,1)} %get-tuple-element.40) | copy-start | bytes 6291460
  23.6 35.5 %collective-permute-start.1 = (bf16[768,1024]{1,0:T(8,128)(2,1)S(1)}, bf16[768,1024]{1,0:T(8,128)(2,1)S(1)}, u32[]{:S(2)}, u32[]{:S(2)}) collective-permute-start(bf16[768,1024]{1,0:T(8,128)(2,1)S(1)} %slice.20), channel_id=1, source_target_pairs={{0,8},{8,0},{1,9},{9,1},{2,10},{10,2},{3,11},{11,3},{4,12},{12,4},... | collective-permute-start | bytes 4718600 | tf_op jit(solution)/shard_map/ppermute | solution.py:200
  41.9 6.8 %copy-start.3 = (bf16[1024,1024]{1,0:T(8,128)(2,1)S(1)}, bf16[1024,1024]{1,0:T(8,128)(2,1)}, u32[]{:S(2)}) copy-start(bf16[1024,1024]{1,0:T(8,128)(2,1)} %get-tuple-element.31) | copy-start | bytes 6291460
  41.9 42.2 %collective-permute-start.5 = (bf16[256,1024]{1,0:T(8,128)(2,1)S(1)}, bf16[256,1024]{1,0:T(8,128)(2,1)S(1)}, u32[]{:S(2)}, u32[]{:S(2)}) collective-permute-start(bf16[256,1024]{1,0:T(8,128)(2,1)S(1)} %slice_select_fusion), channel_id=1, source_target_pairs={{0,4},{1,5},{2,6},{3,7},{4,0},{5,1},{6,2},{7,3},{8,12},{9,13},{10,... | collective-permute-start | bytes 1572872 | tf_op jit(solution)/shard_map/ppermute | solution.py:204
  42.5 33.6 %collective-permute-start.10 = (bf16[512,1024]{1,0:T(8,128)(2,1)S(1)}, bf16[512,1024]{1,0:T(8,128)(2,1)S(1)}, u32[]{:S(2)}, u32[]{:S(2)}) collective-permute-start(bf16[512,1024]{1,0:T(8,128)(2,1)S(1)} %pad_maximum_fusion), channel_id=1, source_target_pairs={{0,1},{1,0},{2,3},{3,2},{4,5},{5,4},{6,7},{7,6},{8,9},{9,8},{10,11... | collective-permute-start | bytes 3145736 | tf_op jit(solution)/shard_map/ppermute | solution.py:201
  51.8 7.4 %copy-start.1 = (bf16[1,1024,1024]{2,1,0:T(8,128)(2,1)S(1)}, bf16[1,1024,1024]{2,1,0:T(8,128)(2,1)}, u32[]{:S(2)}) copy-start(bf16[1,1024,1024]{2,1,0:T(8,128)(2,1)} %param.4) | copy-start | bytes 6291460
  64.3 9.4 %copy-start.5 = (bf16[1024,1024]{1,0:T(8,128)(2,1)S(1)}, bf16[1024,1024]{1,0:T(8,128)(2,1)}, u32[]{:S(2)}) copy-start(bf16[1024,1024]{1,0:T(8,128)(2,1)} %get-tuple-element.26) | copy-start | bytes 6291460
  64.3 35.9 %collective-permute-start.9 = (bf16[512,1024]{1,0:T(8,128)(2,1)S(1)}, bf16[512,1024]{1,0:T(8,128)(2,1)S(1)}, u32[]{:S(2)}, u32[]{:S(2)}) collective-permute-start(bf16[512,1024]{1,0:T(8,128)(2,1)S(1)} %maximum_select_fusion), channel_id=1, source_target_pairs={{0,1},{1,0},{2,3},{3,2},{4,5},{5,4},{6,7},{7,6},{8,9},{9,8},{10,11... | collective-permute-start | bytes 3145736 | tf_op jit(solution)/shard_map/ppermute | solution.py:201
  64.4 30.6 %collective-permute-start.4 = (bf16[512,1024]{1,0:T(8,128)(2,1)S(1)}, bf16[512,1024]{1,0:T(8,128)(2,1)S(1)}, u32[]{:S(2)}, u32[]{:S(2)}) collective-permute-start(bf16[512,1024]{1,0:T(8,128)(2,1)S(1)} %pad_maximum_fusion), channel_id=1, source_target_pairs={{0,8},{8,0},{1,9},{9,1},{2,10},{10,2},{3,11},{11,3},{4,12},{12,4},... | collective-permute-start | bytes 3145736 | tf_op jit(solution)/shard_map/ppermute | solution.py:200
  81.4 28.1 %collective-permute-start.7 = (bf16[768,1024]{1,0:T(8,128)(2,1)S(1)}, bf16[768,1024]{1,0:T(8,128)(2,1)S(1)}, u32[]{:S(2)}, u32[]{:S(2)}) collective-permute-start(bf16[768,1024]{1,0:T(8,128)(2,1)S(1)} %collective-permute-done.1), channel_id=1, source_target_pairs={{0,1},{9,8},{1,2},{10,9},{2,3},{11,10},{3,4},{12,11},{4,5},{13,12}... | collective-permute-start | bytes 4718600 | tf_op jit(solution)/shard_map/ppermute | solution.py:209
  95.0 9.3 %collective-permute-start.11 = (bf16[256,1024]{1,0:T(8,128)(2,1)S(1)}, bf16[256,1024]{1,0:T(8,128)(2,1)S(1)}, u32[]{:S(2)}, u32[]{:S(2)}) collective-permute-start(bf16[256,1024]{1,0:T(8,128)(2,1)S(1)} %collective-permute-done.5), channel_id=1, source_target_pairs={{0,1},{1,0},{2,3},{3,2},{4,5},{5,4},{6,7},{7,6},{8,9},{9,8},{10,11... | collective-permute-start | bytes 1572872 | tf_op jit(solution)/shard_map/ppermute | solution.py:201
  96.0 13.6 %collective-permute-start.6 = (bf16[256,1024]{1,0:T(8,128)(2,1)S(1)}, bf16[256,1024]{1,0:T(8,128)(2,1)S(1)}, u32[]{:S(2)}, u32[]{:S(2)}) collective-permute-start(bf16[256,1024]{1,0:T(8,128)(2,1)S(1)} %collective-permute-done.5), channel_id=1, source_target_pairs={{0,8},{8,0},{1,9},{9,1},{2,10},{10,2},{3,11},{11,3},{4,12},{12,4},... | collective-permute-start | bytes 1572872 | tf_op jit(solution)/shard_map/ppermute | solution.py:200
  97.4 18.1 %collective-permute-start.12 = (bf16[512,1024]{1,0:T(8,128)(2,1)S(1)}, bf16[512,1024]{1,0:T(8,128)(2,1)S(1)}, u32[]{:S(2)}, u32[]{:S(2)}) collective-permute-start(bf16[512,1024]{1,0:T(8,128)(2,1)S(1)} %collective-permute-done.4), channel_id=1, source_target_pairs={{0,1},{1,0},{2,3},{3,2},{4,5},{5,4},{6,7},{7,6},{8,9},{9,8},{10,11... | collective-permute-start | bytes 3145736 | tf_op jit(solution)/shard_map/ppermute | solution.py:201
  111.0 7.3 %collective-permute-start.13 = (bf16[256,1024]{1,0:T(8,128)(2,1)S(1)}, bf16[256,1024]{1,0:T(8,128)(2,1)S(1)}, u32[]{:S(2)}, u32[]{:S(2)}) collective-permute-start(bf16[256,1024]{1,0:T(8,128)(2,1)S(1)} %collective-permute-done.6), channel_id=1, source_target_pairs={{0,1},{1,0},{2,3},{3,2},{4,5},{5,4},{6,7},{7,6},{8,9},{9,8},{10,11... | collective-permute-start | bytes 1572872 | tf_op jit(solution)/shard_map/ppermute | solution.py:201
where the time goes:
time: 468 us
  Pallas kernels  353 us (75%)
  matrix products  42 us (9%)
  waiting for transfers between devices  40.5 us (9%)
  starting transfers between devices  26.1 us (6%)
    pallas_call x1, Pallas kernels, attend(): pl.pallas_call(functools.partial(attend_kernel, blocks, count, chunk, tog...  344 us
    ppermute x4, waiting for transfers between devices, rows_by_axes(): swap = lambda rows: lax.ppermute(rows, 'head', [(0, 1), (1, 0)])  23.7 us
    dot_general x15, matrix products, project_columns(): lax.dot_general(weight, rows, (((1,), (1,)), ((), ())), preferred_element...  20.8 us
    dot_general x14, matrix products, project_rows(): jnp.dot(rows, weight, preferred_element_type=jnp.float32)  17.6 us
    ppermute x3, waiting for transfers between devices, along(): lax.ppermute(rows, 'blk', [(s, (s + 2 * k) % strides) for s in range(stri...  16.8 us
    ppermute x4, starting transfers between devices, rows_by_axes(): swap = lambda rows: lax.ppermute(rows, 'head', [(0, 1), (1, 0)])  10.3 us
  transfers between devices with their start and end apart: 14, of which 6 were waited for; matrix products, arithmetic and copies ran while one was open for 9% of the time, Pallas kernels for 2%

commit v1 on v0

--- a/solution.py
+++ b/solution.py
@@ -18,7 +18,7 @@
 KSEL = 16
 PAIRS = H // 2
 LANES = 2 * HD
-TOTAL_CAP = 2.0**100
+TOTAL_CAP = 2.0**12
 
 
 def split_kernel(weight_ref, query_ref, key_ref, value_ref):
@@ -120,7 +120,7 @@
         total = None
         shift = shift_ref[pl.ds(index, 1), :]
         for which in range(0, count, chunk):
-            raised = jnp.exp(score(index, which, chunk, query) - shift).astype(bf16)
+            raised = jnp.exp((score(index, which, chunk, query) - shift).astype(bf16))
             part = gather(index, which, chunk, raised)
             total = part if total is None else total + part
         return finish(index, total)

time: 468 us -> 467 us (level)
  no operation moved by 1% of the time
where the time goes in v1:
time: 467 us; the launch traced here: 466 us
  Pallas kernels  352 us (75%)
  matrix products  42 us (9%)
  waiting for transfers between devices  40.5 us (9%)
  starting transfers between devices  26.1 us (6%)
    pallas_call x1, Pallas kernels, attend(): pl.pallas_call(functools.partial(attend_kernel, blocks, count, chunk, tog...  343 us
    ppermute x4, waiting for transfers between devices, rows_by_axes(): swap = lambda rows: lax.ppermute(rows, 'head', [(0, 1), (1, 0)])  23.7 us
    dot_general x15, matrix products, project_columns(): lax.dot_general(weight, rows, (((1,), (1,)), ((), ())), preferred_element...  20.8 us
    dot_general x14, matrix products, project_rows(): jnp.dot(rows, weight, preferred_element_type=jnp.float32)  17.6 us
    ppermute x3, waiting for transfers between devices, along(): lax.ppermute(rows, 'blk', [(s, (s + 2 * k) % strides) for s in range(stri...  16.8 us
    ppermute x4, starting transfers between devices, rows_by_axes(): swap = lambda rows: lax.ppermute(rows, 'head', [(0, 1), (1, 0)])  10.3 us
  transfers between devices with their start and end apart: 14, of which 6 were waited for; matrix products, arithmetic and copies ran while one was open for 9% of the time, Pallas kernels for 2%

profile of v1, /device:TPU:11, one launch (start us, length us, event | category | flops | bytes accessed | tf_op | source)
XLA Modules:
  0.0 466.4 jit_solution(8353430270947469474)
XLA Ops:
  1.2 1.3 collective-permute-start
  2.5 8.6 %split_weights.1 = (bf16[1024,1024]{1,0:T(8,128)(2,1)}, bf16[1024,1024]{1,0:T(8,128)(2,1)}, bf16[1024,1024]{1,0:T(8,128)(2,1)}) custom-call(bf16[1024,3072]{1,0:T(8,128)(2,1)} %weight_ref.1), custom_call_target="tpu_custom_call" | custom-call | bytes 12582912 | tf_op jit(solution)/shard_map/split_weights/pallas_call | solution.py:41
  11.1 3.0 collective-permute-done
  15.4 1.3 collective-permute-start.2
  16.7 5.2 %collective-permute-start.8 = (bf16[256,1024]{1,0:T(8,128)(2,1)S(1)}, bf16[256,1024]{1,0:T(8,128)(2,1)}, u32[]{:S(2)}, u32[]{:S(2)}) collective-permute-start(bf16[256,1024]{1,0:T(8,128)(2,1)S(1)} %collective-permute-done), channel_id=1, source_target_pairs={{0,1},{9,8},{1,2},{10,9},{2,3},{11,10},{3,4},{12,11},{4,5},{13,12}... | collective-permute-start | bytes 1572872 | tf_op jit(solution)/shard_map/ppermute | solution.py:209
  22.0 1.7 slice.20
  23.8 3.4 collective-permute-done.3
  27.2 13.3 %collective-permute-done.2 = bf16[256,1024]{1,0:T(8,128)(2,1)} collective-permute-done((bf16[256,1024]{1,0:T(8,128)(2,1)S(1)}, bf16[256,1024]{1,0:T(8,128)(2,1)}, u32[]{:S(2)}, u32[]{:S(2)}) %collective-permute-start.2) | collective-permute-done | bytes 524320 | tf_op jit(solution)/shard_map/ppermute | solution.py:204
  40.6 1.3 pad_maximum_fusion
  42.5 4.4 collective-permute-start.10
  46.9 1.8 convolution_convert_fusion.20.refs_18_
  48.7 1.8 convolution_convert_fusion.26.refs_4_
  50.5 1.3 convolution_convert_fusion.9.refs_20_
  53.0 6.1 %collective-permute-done.1 = bf16[768,1024]{1,0:T(8,128)(2,1)S(1)} collective-permute-done((bf16[768,1024]{1,0:T(8,128)(2,1)S(1)}, bf16[768,1024]{1,0:T(8,128)(2,1)S(1)}, u32[]{:S(2)}, u32[]{:S(2)}) %collective-permute-start.1) | collective-permute-done | bytes 1572896 | tf_op jit(solution)/shard_map/ppermute | solution.py:200
  59.1 2.3 convolution_convert_fusion.1.refs_0_
  61.5 2.4 convolution_convert_fusion.refs_14_
  64.4 7.4 %collective-permute-start.4 = (bf16[512,1024]{1,0:T(8,128)(2,1)S(1)}, bf16[512,1024]{1,0:T(8,128)(2,1)S(1)}, u32[]{:S(2)}, u32[]{:S(2)}) collective-permute-start(bf16[512,1024]{1,0:T(8,128)(2,1)S(1)} %pad_maximum_fusion), channel_id=1, source_target_pairs={{0,8},{8,0},{1,9},{9,1},{2,10},{10,2},{3,11},{11,3},{4,12},{12,4},... | collective-permute-start | bytes 3145736 | tf_op jit(solution)/shard_map/ppermute | solution.py:200
  71.9 1.8 convolution_convert_fusion.3.refs_15_
  73.7 2.4 multiply_convert_fusion.query_ref
  76.1 1.5 convolution_convert_fusion.8.refs_22_
  78.9 1.8 convolution_convert_fusion.5.refs_1_
  81.4 1.9 collective-permute-start.7
  84.1 10.9 %collective-permute-done.4 = bf16[512,1024]{1,0:T(8,128)(2,1)S(1)} collective-permute-done((bf16[512,1024]{1,0:T(8,128)(2,1)S(1)}, bf16[512,1024]{1,0:T(8,128)(2,1)S(1)}, u32[]{:S(2)}, u32[]{:S(2)}) %collective-permute-start.4) | collective-permute-done | bytes 1048608 | tf_op jit(solution)/shard_map/ppermute | solution.py:200
  96.0 1.5 collective-permute-start.6
  97.7 1.3 convolution_convert_fusion.7.refs_24_
  100.3 1.3 convolution_convert_fusion.10.refs_19_
  105.8 3.7 collective-permute-done.6
  111.9 1.8 convolution_convert_fusion.2.refs_17_
  113.7 1.8 convolution_convert_fusion.4.refs_3_
  115.5 1.5 convolution_convert_fusion.6.refs_26_
  119.8 342.9 %attend.1 = bf16[1024,1024]{1,0:T(8,128)(2,1)S(1)} custom-call(s32[8,16]{1,0:T(8,128)S(1)} %fusion.6.table_ref, bf16[1024,1024]{1,0:T(8,128)(2,1)S(1)} %multiply_convert_fusion.query_ref, bf16[1024,1024]{1,0:T(8,128)(2,1)S(1)} %convolution_convert_fusion.1.refs_0_, bf16[768,1024]{1,0:T(8,128)(2,1)S(1)} %convolution_convert_fusion.5.refs_1_, ...), custom_call_target="tpu_custom_call" | custom-call | flops 51539607552 | bytes 31457280 | tf_op jit(solution)/shard_map/attend/pallas_call | solution.py:164
  462.8 3.7 convert_bitcast_fusion
  (48 shorter events, 19.7 us)
Async XLA Ops:
  0.0 462.7 %copy-start = (bf16[1024,1024]{1,0:T(8,128)(2,1)S(1)}, bf16[1024,1024]{1,0:T(8,128)(2,1)}, u32[]{:S(2)}) copy-start(bf16[1024,1024]{1,0:T(8,128)(2,1)} %param.6) | copy-start | bytes 6291460
  1.2 12.9 %collective-permute-start = (bf16[256,1024]{1,0:T(8,128)(2,1)S(1)}, bf16[256,1024]{1,0:T(8,128)(2,1)S(1)}, u32[]{:S(2)}, u32[]{:S(2)}) collective-permute-start(bf16[256,1024]{1,0:T(8,128)(2,1)S(1)} %slice_bitcast_fusion), channel_id=1, source_target_pairs={{0,8},{8,0},{1,9},{9,1},{2,10},{10,2},{3,11},{11,3},{4,12},{12,4},... | collective-permute-start | bytes 1572872 | tf_op jit(solution)/shard_map/ppermute | solution.py:200
  14.1 9.7 %copy-start.2 = (s32[16,16]{1,0:T(8,128)S(1)}, s32[16,16]{1,0:T(8,128)}, u32[]{:S(2)}) copy-start(s32[16,16]{1,0:T(8,128)} %param.7) | copy-start | bytes 3076
  15.2 12.0 %collective-permute-start.3 = (bf16[256,1024]{1,0:T(8,128)(2,1)S(1)}, bf16[256,1024]{1,0:T(8,128)(2,1)}, u32[]{:S(2)}, u32[]{:S(2)}) collective-permute-start(bf16[256,1024]{1,0:T(8,128)(2,1)S(1)} %slice_select_fusion), channel_id=1, source_target_pairs={{0,6},{1,7},{2,0},{3,1},{4,2},{5,3},{6,4},{7,5},{8,14},{9,15},{10,... | collective-permute-start | bytes 1572872 | tf_op jit(solution)/shard_map/ppermute | solution.py:204
  15.4 25.2 %collective-permute-start.2 = (bf16[256,1024]{1,0:T(8,128)(2,1)S(1)}, bf16[256,1024]{1,0:T(8,128)(2,1)}, u32[]{:S(2)}, u32[]{:S(2)}) collective-permute-start(bf16[256,1024]{1,0:T(8,128)(2,1)S(1)} %slice_select_fusion), channel_id=1, source_target_pairs={{0,2},{1,3},{2,4},{3,5},{4,6},{5,7},{6,0},{7,1},{8,10},{9,11},{10,... | collective-permute-start | bytes 1572872 | tf_op jit(solution)/shard_map/ppermute | solution.py:204
  16.7 30.2 %collective-permute-start.8 = (bf16[256,1024]{1,0:T(8,128)(2,1)S(1)}, bf16[256,1024]{1,0:T(8,128)(2,1)}, u32[]{:S(2)}, u32[]{:S(2)}) collective-permute-start(bf16[256,1024]{1,0:T(8,128)(2,1)S(1)} %collective-permute-done), channel_id=1, source_target_pairs={{0,1},{9,8},{1,2},{10,9},{2,3},{11,10},{3,4},{12,11},{4,5},{13,12}... | collective-permute-start | bytes 1572872 | tf_op jit(solution)/shard_map/ppermute | solution.py:209
  21.9 24.9 %copy-start.4 = (bf16[1024,1024]{1,0:T(8,128)(2,1)S(1)}, bf16[1024,1024]{1,0:T(8,128)(2,1)}, u32[]{:S(2)}) copy-start(bf16[1024,1024]{1,0:T(8,128)(2,1)} %get-tuple-element.40) | copy-start | bytes 6291460
  23.6 35.5 %collective-permute-start.1 = (bf16[768,1024]{1,0:T(8,128)(2,1)S(1)}, bf16[768,1024]{1,0:T(8,128)(2,1)S(1)}, u32[]{:S(2)}, u32[]{:S(2)}) collective-permute-start(bf16[768,1024]{1,0:T(8,128)(2,1)S(1)} %slice.20), channel_id=1, source_target_pairs={{0,8},{8,0},{1,9},{9,1},{2,10},{10,2},{3,11},{11,3},{4,12},{12,4},... | collective-permute-start | bytes 4718600 | tf_op jit(solution)/shard_map/ppermute | solution.py:200
  41.9 6.8 %copy-start.3 = (bf16[1024,1024]{1,0:T(8,128)(2,1)S(1)}, bf16[1024,1024]{1,0:T(8,128)(2,1)}, u32[]{:S(2)}) copy-start(bf16[1024,1024]{1,0:T(8,128)(2,1)} %get-tuple-element.31) | copy-start | bytes 6291460
  41.9 42.2 %collective-permute-start.5 = (bf16[256,1024]{1,0:T(8,128)(2,1)S(1)}, bf16[256,1024]{1,0:T(8,128)(2,1)S(1)}, u32[]{:S(2)}, u32[]{:S(2)}) collective-permute-start(bf16[256,1024]{1,0:T(8,128)(2,1)S(1)} %slice_select_fusion), channel_id=1, source_target_pairs={{0,4},{1,5},{2,6},{3,7},{4,0},{5,1},{6,2},{7,3},{8,12},{9,13},{10,... | collective-permute-start | bytes 1572872 | tf_op jit(solution)/shard_map/ppermute | solution.py:204
  42.5 33.6 %collective-permute-start.10 = (bf16[512,1024]{1,0:T(8,128)(2,1)S(1)}, bf16[512,1024]{1,0:T(8,128)(2,1)S(1)}, u32[]{:S(2)}, u32[]{:S(2)}) collective-permute-start(bf16[512,1024]{1,0:T(8,128)(2,1)S(1)} %pad_maximum_fusion), channel_id=1, source_target_pairs={{0,1},{1,0},{2,3},{3,2},{4,5},{5,4},{6,7},{7,6},{8,9},{9,8},{10,11... | collective-permute-start | bytes 3145736 | tf_op jit(solution)/shard_map/ppermute | solution.py:201
  51.8 7.4 %copy-start.1 = (bf16[1,1024,1024]{2,1,0:T(8,128)(2,1)S(1)}, bf16[1,1024,1024]{2,1,0:T(8,128)(2,1)}, u32[]{:S(2)}) copy-start(bf16[1,1024,1024]{2,1,0:T(8,128)(2,1)} %param.4) | copy-start | bytes 6291460
  64.3 9.4 %copy-start.5 = (bf16[1024,1024]{1,0:T(8,128)(2,1)S(1)}, bf16[1024,1024]{1,0:T(8,128)(2,1)}, u32[]{:S(2)}) copy-start(bf16[1024,1024]{1,0:T(8,128)(2,1)} %get-tuple-element.26) | copy-start | bytes 6291460
  64.3 35.9 %collective-permute-start.9 = (bf16[512,1024]{1,0:T(8,128)(2,1)S(1)}, bf16[512,1024]{1,0:T(8,128)(2,1)S(1)}, u32[]{:S(2)}, u32[]{:S(2)}) collective-permute-start(bf16[512,1024]{1,0:T(8,128)(2,1)S(1)} %maximum_select_fusion), channel_id=1, source_target_pairs={{0,1},{1,0},{2,3},{3,2},{4,5},{5,4},{6,7},{7,6},{8,9},{9,8},{10,11... | collective-permute-start | bytes 3145736 | tf_op jit(solution)/shard_map/ppermute | solution.py:201
  64.4 30.6 %collective-permute-start.4 = (bf16[512,1024]{1,0:T(8,128)(2,1)S(1)}, bf16[512,1024]{1,0:T(8,128)(2,1)S(1)}, u32[]{:S(2)}, u32[]{:S(2)}) collective-permute-start(bf16[512,1024]{1,0:T(8,128)(2,1)S(1)} %pad_maximum_fusion), channel_id=1, source_target_pairs={{0,8},{8,0},{1,9},{9,1},{2,10},{10,2},{3,11},{11,3},{4,12},{12,4},... | collective-permute-start | bytes 3145736 | tf_op jit(solution)/shard_map/ppermute | solution.py:200
  81.4 28.1 %collective-permute-start.7 = (bf16[768,1024]{1,0:T(8,128)(2,1)S(1)}, bf16[768,1024]{1,0:T(8,128)(2,1)S(1)}, u32[]{:S(2)}, u32[]{:S(2)}) collective-permute-start(bf16[768,1024]{1,0:T(8,128)(2,1)S(1)} %collective-permute-done.1), channel_id=1, source_target_pairs={{0,1},{9,8},{1,2},{10,9},{2,3},{11,10},{3,4},{12,11},{4,5},{13,12}... | collective-permute-start | bytes 4718600 | tf_op jit(solution)/shard_map/ppermute | solution.py:209
  95.0 9.3 %collective-permute-start.11 = (bf16[256,1024]{1,0:T(8,128)(2,1)S(1)}, bf16[256,1024]{1,0:T(8,128)(2,1)S(1)}, u32[]{:S(2)}, u32[]{:S(2)}) collective-permute-start(bf16[256,1024]{1,0:T(8,128)(2,1)S(1)} %collective-permute-done.5), channel_id=1, source_target_pairs={{0,1},{1,0},{2,3},{3,2},{4,5},{5,4},{6,7},{7,6},{8,9},{9,8},{10,11... | collective-permute-start | bytes 1572872 | tf_op jit(solution)/shard_map/ppermute | solution.py:201
  96.0 13.6 %collective-permute-start.6 = (bf16[256,1024]{1,0:T(8,128)(2,1)S(1)}, bf16[256,1024]{1,0:T(8,128)(2,1)S(1)}, u32[]{:S(2)}, u32[]{:S(2)}) collective-permute-start(bf16[256,1024]{1,0:T(8,128)(2,1)S(1)} %collective-permute-done.5), channel_id=1, source_target_pairs={{0,8},{8,0},{1,9},{9,1},{2,10},{10,2},{3,11},{11,3},{4,12},{12,4},... | collective-permute-start | bytes 1572872 | tf_op jit(solution)/shard_map/ppermute | solution.py:200
  97.4 18.1 %collective-permute-start.12 = (bf16[512,1024]{1,0:T(8,128)(2,1)S(1)}, bf16[512,1024]{1,0:T(8,128)(2,1)S(1)}, u32[]{:S(2)}, u32[]{:S(2)}) collective-permute-start(bf16[512,1024]{1,0:T(8,128)(2,1)S(1)} %collective-permute-done.4), channel_id=1, source_target_pairs={{0,1},{1,0},{2,3},{3,2},{4,5},{5,4},{6,7},{7,6},{8,9},{9,8},{10,11... | collective-permute-start | bytes 3145736 | tf_op jit(solution)/shard_map/ppermute | solution.py:201
  111.0 7.3 %collective-permute-start.13 = (bf16[256,1024]{1,0:T(8,128)(2,1)S(1)}, bf16[256,1024]{1,0:T(8,128)(2,1)S(1)}, u32[]{:S(2)}, u32[]{:S(2)}) collective-permute-start(bf16[256,1024]{1,0:T(8,128)(2,1)S(1)} %collective-permute-done.6), channel_id=1, source_target_pairs={{0,1},{1,0},{2,3},{3,2},{4,5},{5,4},{6,7},{7,6},{8,9},{9,8},{10,11... | collective-permute-start | bytes 1572872 | tf_op jit(solution)/shard_map/ppermute | solution.py:201

commit v2 on v0

--- a/solution.py
+++ b/solution.py
@@ -216,13 +216,13 @@
     ends = [along(carried, 1), along(carried, chips - 1)]
     ends, after = lax.optimization_barrier((jnp.concatenate(ends, axis=0), carried))
     middle = jnp.concatenate([along(after, k) for k in range(2, chips - 1)], axis=0)
-    own, other, other_end, released = lax.optimization_barrier((own, other, other_end, ends))
+    other, other_end, released = lax.optimization_barrier((other, other_end, ends))
     across_ends = swap(released)
     edge = to_next(other)
+    nearby = jnp.where(low, jnp.concatenate([other_end, other[-half:]], axis=0), own[cut:])
+    across_ends, middle, own = lax.optimization_barrier((across_ends, middle, own))
     query = project_columns(weights[0], own, HD**-0.5)
-    across_ends, middle = lax.optimization_barrier((across_ends, middle))
-    across_middle, edge = lax.optimization_barrier((swap(middle), edge))
-    nearby = jnp.where(low, jnp.concatenate([other_end, other[-half:]], axis=0), own[cut:])
+    across_middle = swap(middle)
     pieces = [own, other, other_end, edge, edge_end, beside(nearby)]
     pieces += [ends, middle, beside(ends), beside(middle)]
     pieces += [across_ends, across_middle, beside(across_ends), beside(across_middle)]

time: 468 us -> 467 us (level)
  waiting for transfers between devices: 40.5 us -> 35.8 us
    ppermute x4, waiting for transfers between devices: 23.7 us -> 19 us  [rows_by_axes(): swap = lambda rows: lax.ppermute(rows, 'head', [(0, 1), (1, 0)])]
  transfers between devices with their start and end apart: 14 -> 14, of which waited for: 6 -> 5; matrix products, arithmetic and copies ran while one was open for 9% -> 8% of each run, Pallas kernels for 2% -> 2%
where the time goes in v2:
time: 467 us; the launch traced here: 463 us
  Pallas kernels  353 us (76%)
  matrix products  42.1 us (9%)
  waiting for transfers between devices  35.8 us (8%)
  starting transfers between devices  25.2 us (5%)
    pallas_call x1, Pallas kernels, attend(): pl.pallas_call(functools.partial(attend_kernel, blocks, count, chunk, tog...  344 us
    dot_general x15, matrix products, project_columns(): lax.dot_general(weight, rows, (((1,), (1,)), ((), ())), preferred_element...  20.9 us
    ppermute x4, waiting for transfers between devices, rows_by_axes(): swap = lambda rows: lax.ppermute(rows, 'head', [(0, 1), (1, 0)])  19 us
    dot_general x14, matrix products, project_rows(): jnp.dot(rows, weight, preferred_element_type=jnp.float32)  17.6 us
    ppermute x3, waiting for transfers between devices, along(): lax.ppermute(rows, 'blk', [(s, (s + 2 * k) % strides) for s in range(stri...  16.8 us
    ppermute x4, starting transfers between devices, rows_by_axes(): swap = lambda rows: lax.ppermute(rows, 'head', [(0, 1), (1, 0)])  10.7 us
  transfers between devices with their start and end apart: 14, of which 5 were waited for; matrix products, arithmetic and copies ran while one was open for 8% of the time, Pallas kernels for 2%

profile of v2, /device:TPU:11, one launch (start us, length us, event | category | flops | bytes accessed | tf_op | source)
XLA Modules:
  0.0 463.2 jit_solution(10439301955096075781)
XLA Ops:
  1.2 1.3 collective-permute-start
  2.5 8.6 %split_weights.1 = (bf16[1024,1024]{1,0:T(8,128)(2,1)}, bf16[1024,1024]{1,0:T(8,128)(2,1)}, bf16[1024,1024]{1,0:T(8,128)(2,1)}) custom-call(bf16[1024,3072]{1,0:T(8,128)(2,1)} %weight_ref.1), custom_call_target="tpu_custom_call" | custom-call | bytes 12582912 | tf_op jit(solution)/shard_map/split_weights/pallas_call | solution.py:41
  11.1 3.0 collective-permute-done
  15.4 1.3 collective-permute-start.2
  16.7 5.2 %collective-permute-start.7 = (bf16[256,1024]{1,0:T(8,128)(2,1)S(1)}, bf16[256,1024]{1,0:T(8,128)(2,1)}, u32[]{:S(2)}, u32[]{:S(2)}) collective-permute-start(bf16[256,1024]{1,0:T(8,128)(2,1)S(1)} %collective-permute-done), channel_id=1, source_target_pairs={{0,1},{9,8},{1,2},{10,9},{2,3},{11,10},{3,4},{12,11},{4,5},{13,12}... | collective-permute-start | bytes 1572872 | tf_op jit(solution)/shard_map/ppermute | solution.py:209
  22.0 1.7 slice.20
  23.8 3.4 collective-permute-done.3
  27.2 13.3 %collective-permute-done.2 = bf16[256,1024]{1,0:T(8,128)(2,1)} collective-permute-done((bf16[256,1024]{1,0:T(8,128)(2,1)S(1)}, bf16[256,1024]{1,0:T(8,128)(2,1)}, u32[]{:S(2)}, u32[]{:S(2)}) %collective-permute-start.2) | collective-permute-done | bytes 524320 | tf_op jit(solution)/shard_map/ppermute | solution.py:204
  40.6 1.3 pad_maximum_fusion
  42.5 4.4 collective-permute-start.9
  46.9 1.8 convolution_convert_fusion.20.refs_18_
  48.7 1.3 convolution_convert_fusion.9.refs_20_
  51.5 1.8 convolution_convert_fusion.26.refs_4_
  53.3 5.8 %collective-permute-done.1 = bf16[768,1024]{1,0:T(8,128)(2,1)S(1)} collective-permute-done((bf16[768,1024]{1,0:T(8,128)(2,1)S(1)}, bf16[768,1024]{1,0:T(8,128)(2,1)S(1)}, u32[]{:S(2)}, u32[]{:S(2)}) %collective-permute-start.1) | collective-permute-done | bytes 1572896 | tf_op jit(solution)/shard_map/ppermute | solution.py:200
  59.2 2.1 collective-permute-start.6
  61.3 7.4 %collective-permute-start.4 = (bf16[512,1024]{1,0:T(8,128)(2,1)S(1)}, bf16[512,1024]{1,0:T(8,128)(2,1)S(1)}, u32[]{:S(2)}, u32[]{:S(2)}) collective-permute-start(bf16[512,1024]{1,0:T(8,128)(2,1)S(1)} %pad_maximum_fusion), channel_id=1, source_target_pairs={{0,8},{8,0},{1,9},{9,1},{2,10},{10,2},{3,11},{11,3},{4,12},{12,4},... | collective-permute-start | bytes 3145736 | tf_op jit(solution)/shard_map/ppermute | solution.py:200
  69.4 1.8 convolution_convert_fusion.3.refs_15_
  71.3 1.3 convolution_convert_fusion.8.refs_22_
  72.6 1.3 convolution_convert_fusion.13.refs_8_
  76.0 1.8 convolution_convert_fusion.5.refs_1_
  77.8 10.2 %collective-permute-done.4 = bf16[512,1024]{1,0:T(8,128)(2,1)S(1)} collective-permute-done((bf16[512,1024]{1,0:T(8,128)(2,1)S(1)}, bf16[512,1024]{1,0:T(8,128)(2,1)S(1)}, u32[]{:S(2)}, u32[]{:S(2)}) %collective-permute-start.4) | collective-permute-done | bytes 1048608 | tf_op jit(solution)/shard_map/ppermute | solution.py:200
  88.7 1.8 collective-permute-start.11
  90.5 1.3 convolution_convert_fusion.7.refs_24_
  93.7 2.3 convolution_convert_fusion.1.refs_0_
  96.0 2.6 convolution_convert_fusion.refs_14_
  98.7 2.4 multiply_convert_fusion.query_ref
  101.0 1.3 convolution_convert_fusion.10.refs_19_
  107.4 1.8 convolution_convert_fusion.2.refs_17_
  109.2 1.8 convolution_convert_fusion.4.refs_3_
  112.6 1.6 convolution_convert_fusion.6.refs_26_
  115.4 344.2 %attend.1 = bf16[1024,1024]{1,0:T(8,128)(2,1)S(1)} custom-call(s32[8,16]{1,0:T(8,128)S(1)} %fusion.6.table_ref, bf16[1024,1024]{1,0:T(8,128)(2,1)S(1)} %multiply_convert_fusion.query_ref, bf16[1024,1024]{1,0:T(8,128)(2,1)S(1)} %convolution_convert_fusion.1.refs_0_, bf16[768,1024]{1,0:T(8,128)(2,1)S(1)} %convolution_convert_fusion.5.refs_1_, ...), custom_call_target="tpu_custom_call" | custom-call | flops 51539607552 | bytes 31457280 | tf_op jit(solution)/shard_map/attend/pallas_call | solution.py:164
  459.6 3.7 convert_bitcast_fusion
  (48 shorter events, 18.1 us)
Async XLA Ops:
  0.0 459.6 %copy-start = (bf16[1024,1024]{1,0:T(8,128)(2,1)S(1)}, bf16[1024,1024]{1,0:T(8,128)(2,1)}, u32[]{:S(2)}) copy-start(bf16[1024,1024]{1,0:T(8,128)(2,1)} %param.6) | copy-start | bytes 6291460
  1.2 12.9 %collective-permute-start = (bf16[256,1024]{1,0:T(8,128)(2,1)S(1)}, bf16[256,1024]{1,0:T(8,128)(2,1)S(1)}, u32[]{:S(2)}, u32[]{:S(2)}) collective-permute-start(bf16[256,1024]{1,0:T(8,128)(2,1)S(1)} %slice_bitcast_fusion), channel_id=1, source_target_pairs={{0,8},{8,0},{1,9},{9,1},{2,10},{10,2},{3,11},{11,3},{4,12},{12,4},... | collective-permute-start | bytes 1572872 | tf_op jit(solution)/shard_map/ppermute | solution.py:200
  14.1 9.7 %copy-start.2 = (s32[16,16]{1,0:T(8,128)S(1)}, s32[16,16]{1,0:T(8,128)}, u32[]{:S(2)}) copy-start(s32[16,16]{1,0:T(8,128)} %param.7) | copy-start | bytes 3076
  15.2 12.0 %collective-permute-start.3 = (bf16[256,1024]{1,0:T(8,128)(2,1)S(1)}, bf16[256,1024]{1,0:T(8,128)(2,1)}, u32[]{:S(2)}, u32[]{:S(2)}) collective-permute-start(bf16[256,1024]{1,0:T(8,128)(2,1)S(1)} %slice_select_fusion), channel_id=1, source_target_pairs={{0,6},{1,7},{2,0},{3,1},{4,2},{5,3},{6,4},{7,5},{8,14},{9,15},{10,... | collective-permute-start | bytes 1572872 | tf_op jit(solution)/shard_map/ppermute | solution.py:204
  15.4 25.2 %collective-permute-start.2 = (bf16[256,1024]{1,0:T(8,128)(2,1)S(1)}, bf16[256,1024]{1,0:T(8,128)(2,1)}, u32[]{:S(2)}, u32[]{:S(2)}) collective-permute-start(bf16[256,1024]{1,0:T(8,128)(2,1)S(1)} %slice_select_fusion), channel_id=1, source_target_pairs={{0,2},{1,3},{2,4},{3,5},{4,6},{5,7},{6,0},{7,1},{8,10},{9,11},{10,... | collective-permute-start | bytes 1572872 | tf_op jit(solution)/shard_map/ppermute | solution.py:204
  16.7 30.2 %collective-permute-start.7 = (bf16[256,1024]{1,0:T(8,128)(2,1)S(1)}, bf16[256,1024]{1,0:T(8,128)(2,1)}, u32[]{:S(2)}, u32[]{:S(2)}) collective-permute-start(bf16[256,1024]{1,0:T(8,128)(2,1)S(1)} %collective-permute-done), channel_id=1, source_target_pairs={{0,1},{9,8},{1,2},{10,9},{2,3},{11,10},{3,4},{12,11},{4,5},{13,12}... | collective-permute-start | bytes 1572872 | tf_op jit(solution)/shard_map/ppermute | solution.py:209
  21.9 24.9 %copy-start.4 = (bf16[1024,1024]{1,0:T(8,128)(2,1)S(1)}, bf16[1024,1024]{1,0:T(8,128)(2,1)}, u32[]{:S(2)}) copy-start(bf16[1024,1024]{1,0:T(8,128)(2,1)} %get-tuple-element.36) | copy-start | bytes 6291460
  23.6 35.5 %collective-permute-start.1 = (bf16[768,1024]{1,0:T(8,128)(2,1)S(1)}, bf16[768,1024]{1,0:T(8,128)(2,1)S(1)}, u32[]{:S(2)}, u32[]{:S(2)}) collective-permute-start(bf16[768,1024]{1,0:T(8,128)(2,1)S(1)} %slice.20), channel_id=1, source_target_pairs={{0,8},{8,0},{1,9},{9,1},{2,10},{10,2},{3,11},{11,3},{4,12},{12,4},... | collective-permute-start | bytes 4718600 | tf_op jit(solution)/shard_map/ppermute | solution.py:200
  41.9 35.9 %collective-permute-start.5 = (bf16[256,1024]{1,0:T(8,128)(2,1)S(1)}, bf16[256,1024]{1,0:T(8,128)(2,1)S(1)}, u32[]{:S(2)}, u32[]{:S(2)}) collective-permute-start(bf16[256,1024]{1,0:T(8,128)(2,1)S(1)} %slice_select_fusion), channel_id=1, source_target_pairs={{0,4},{1,5},{2,6},{3,7},{4,0},{5,1},{6,2},{7,3},{8,12},{9,13},{10,... | collective-permute-start | bytes 1572872 | tf_op jit(solution)/shard_map/ppermute | solution.py:204
  42.5 28.8 %collective-permute-start.9 = (bf16[512,1024]{1,0:T(8,128)(2,1)S(1)}, bf16[512,1024]{1,0:T(8,128)(2,1)S(1)}, u32[]{:S(2)}, u32[]{:S(2)}) collective-permute-start(bf16[512,1024]{1,0:T(8,128)(2,1)S(1)} %pad_maximum_fusion), channel_id=1, source_target_pairs={{0,1},{1,0},{2,3},{3,2},{4,5},{5,4},{6,7},{7,6},{8,9},{9,8},{10,11... | collective-permute-start | bytes 3145736 | tf_op jit(solution)/shard_map/ppermute | solution.py:201
  48.7 1.6 copy-start.3
  59.2 48.2 %collective-permute-start.6 = (bf16[768,1024]{1,0:T(8,128)(2,1)S(1)}, bf16[768,1024]{1,0:T(8,128)(2,1)S(1)}, u32[]{:S(2)}, u32[]{:S(2)}) collective-permute-start(bf16[768,1024]{1,0:T(8,128)(2,1)S(1)} %collective-permute-done.1), channel_id=1, source_target_pairs={{0,1},{9,8},{1,2},{10,9},{2,3},{11,10},{3,4},{12,11},{4,5},{13,12}... | collective-permute-start | bytes 4718600 | tf_op jit(solution)/shard_map/ppermute | solution.py:209
  61.3 26.7 %collective-permute-start.4 = (bf16[512,1024]{1,0:T(8,128)(2,1)S(1)}, bf16[512,1024]{1,0:T(8,128)(2,1)S(1)}, u32[]{:S(2)}, u32[]{:S(2)}) collective-permute-start(bf16[512,1024]{1,0:T(8,128)(2,1)S(1)} %pad_maximum_fusion), channel_id=1, source_target_pairs={{0,8},{8,0},{1,9},{9,1},{2,10},{10,2},{3,11},{11,3},{4,12},{12,4},... | collective-permute-start | bytes 3145736 | tf_op jit(solution)/shard_map/ppermute | solution.py:200
  73.9 1.6 copy-start.1
  75.9 25.2 %collective-permute-start.8 = (bf16[512,1024]{1,0:T(8,128)(2,1)S(1)}, bf16[512,1024]{1,0:T(8,128)(2,1)S(1)}, u32[]{:S(2)}, u32[]{:S(2)}) collective-permute-start(bf16[512,1024]{1,0:T(8,128)(2,1)S(1)} %maximum_select_fusion), channel_id=1, source_target_pairs={{0,1},{1,0},{2,3},{3,2},{4,5},{5,4},{6,7},{7,6},{8,9},{9,8},{10,11... | collective-permute-start | bytes 3145736 | tf_op jit(solution)/shard_map/ppermute | solution.py:201
  88.7 15.6 %collective-permute-start.11 = (bf16[256,1024]{1,0:T(8,128)(2,1)S(1)}, bf16[256,1024]{1,0:T(8,128)(2,1)S(1)}, u32[]{:S(2)}, u32[]{:S(2)}) collective-permute-start(bf16[256,1024]{1,0:T(8,128)(2,1)S(1)} %collective-permute-done.5), channel_id=1, source_target_pairs={{0,8},{8,0},{1,9},{9,1},{2,10},{10,2},{3,11},{11,3},{4,12},{12,4},... | collective-permute-start | bytes 1572872 | tf_op jit(solution)/shard_map/ppermute | solution.py:200
  90.5 15.4 %collective-permute-start.10 = (bf16[256,1024]{1,0:T(8,128)(2,1)S(1)}, bf16[256,1024]{1,0:T(8,128)(2,1)S(1)}, u32[]{:S(2)}, u32[]{:S(2)}) collective-permute-start(bf16[256,1024]{1,0:T(8,128)(2,1)S(1)} %collective-permute-done.5), channel_id=1, source_target_pairs={{0,1},{1,0},{2,3},{3,2},{4,5},{5,4},{6,7},{7,6},{8,9},{9,8},{10,11... | collective-permute-start | bytes 1572872 | tf_op jit(solution)/shard_map/ppermute | solution.py:201
  93.1 19.5 %collective-permute-start.12 = (bf16[512,1024]{1,0:T(8,128)(2,1)S(1)}, bf16[512,1024]{1,0:T(8,128)(2,1)S(1)}, u32[]{:S(2)}, u32[]{:S(2)}) collective-permute-start(bf16[512,1024]{1,0:T(8,128)(2,1)S(1)} %collective-permute-done.4), channel_id=1, source_target_pairs={{0,1},{1,0},{2,3},{3,2},{4,5},{5,4},{6,7},{7,6},{8,9},{9,8},{10,11... | collective-permute-start | bytes 3145736 | tf_op jit(solution)/shard_map/ppermute | solution.py:201
  96.0 2.6 copy-start.5
  104.3 6.7 %collective-permute-start.13 = (bf16[256,1024]{1,0:T(8,128)(2,1)S(1)}, bf16[256,1024]{1,0:T(8,128)(2,1)S(1)}, u32[]{:S(2)}, u32[]{:S(2)}) collective-permute-start(bf16[256,1024]{1,0:T(8,128)(2,1)S(1)} %collective-permute-done.11), channel_id=1, source_target_pairs={{0,1},{1,0},{2,3},{3,2},{4,5},{5,4},{6,7},{7,6},{8,9},{9,8},{10,11... | collective-permute-start | bytes 1572872 | tf_op jit(solution)/shard_map/ppermute | solution.py:201

commit v3 on v2

--- a/solution.py
+++ b/solution.py
@@ -220,10 +220,11 @@
     across_ends = swap(released)
     edge = to_next(other)
     nearby = jnp.where(low, jnp.concatenate([other_end, other[-half:]], axis=0), own[cut:])
-    across_ends, middle, own = lax.optimization_barrier((across_ends, middle, own))
+    beside_nearby, own = lax.optimization_barrier((beside(nearby), own))
     query = project_columns(weights[0], own, HD**-0.5)
+    across_ends, middle = lax.optimization_barrier((across_ends, middle))
     across_middle = swap(middle)
-    pieces = [own, other, other_end, edge, edge_end, beside(nearby)]
+    pieces = [own, other, other_end, edge, edge_end, beside_nearby]
     pieces += [ends, middle, beside(ends), beside(middle)]
     pieces += [across_ends, across_middle, beside(across_ends), beside(across_middle)]
     span = 2 * (chips - 1)

time: 467 us -> 465 us (level)
  no operation moved by 1% of the time
where the time goes in v3:
time: 465 us; the launch traced here: 464 us
  Pallas kernels  353 us (76%)
  matrix products  42 us (9%)
  waiting for transfers between devices  36.2 us (8%)
  starting transfers between devices  26.9 us (6%)
    pallas_call x1, Pallas kernels, attend(): pl.pallas_call(functools.partial(attend_kernel, blocks, count, chunk, tog...  344 us
    dot_general x15, matrix products, project_columns(): lax.dot_general(weight, rows, (((1,), (1,)), ((), ())), preferred_element...  20.6 us
    ppermute x4, waiting for transfers between devices, rows_by_axes(): swap = lambda rows: lax.ppermute(rows, 'head', [(0, 1), (1, 0)])  19.4 us
    dot_general x14, matrix products, project_rows(): jnp.dot(rows, weight, preferred_element_type=jnp.float32)  17.8 us
    ppermute x3, waiting for transfers between devices, along(): lax.ppermute(rows, 'blk', [(s, (s + 2 * k) % strides) for s in range(stri...  16.8 us
    ppermute x4, starting transfers between devices, rows_by_axes(): swap = lambda rows: lax.ppermute(rows, 'head', [(0, 1), (1, 0)])  10.2 us
  transfers between devices with their start and end apart: 14, of which 5 were waited for; matrix products, arithmetic and copies ran while one was open for 8% of the time, Pallas kernels for 2%

profile of v3, /device:TPU:11, one launch (start us, length us, event | category | flops | bytes accessed | tf_op | source)
XLA Modules:
  0.0 464.4 jit_solution(1481760600249610853)
XLA Ops:
  1.2 1.3 collective-permute-start
  2.5 8.6 %split_weights.1 = (bf16[1024,1024]{1,0:T(8,128)(2,1)}, bf16[1024,1024]{1,0:T(8,128)(2,1)}, bf16[1024,1024]{1,0:T(8,128)(2,1)}) custom-call(bf16[1024,3072]{1,0:T(8,128)(2,1)} %weight_ref.1), custom_call_target="tpu_custom_call" | custom-call | bytes 12582912 | tf_op jit(solution)/shard_map/split_weights/pallas_call | solution.py:41
  11.1 3.0 collective-permute-done
  15.4 1.3 collective-permute-start.2
  16.7 5.2 %collective-permute-start.6 = (bf16[256,1024]{1,0:T(8,128)(2,1)S(1)}, bf16[256,1024]{1,0:T(8,128)(2,1)}, u32[]{:S(2)}, u32[]{:S(2)}) collective-permute-start(bf16[256,1024]{1,0:T(8,128)(2,1)S(1)} %collective-permute-done), channel_id=1, source_target_pairs={{0,1},{9,8},{1,2},{10,9},{2,3},{11,10},{3,4},{12,11},{4,5},{13,12}... | collective-permute-start | bytes 1572872 | tf_op jit(solution)/shard_map/ppermute | solution.py:209
  22.0 1.7 slice.20
  23.8 3.4 collective-permute-done.3
  27.2 13.3 %collective-permute-done.2 = bf16[256,1024]{1,0:T(8,128)(2,1)} collective-permute-done((bf16[256,1024]{1,0:T(8,128)(2,1)S(1)}, bf16[256,1024]{1,0:T(8,128)(2,1)}, u32[]{:S(2)}, u32[]{:S(2)}) %collective-permute-start.2) | collective-permute-done | bytes 524320 | tf_op jit(solution)/shard_map/ppermute | solution.py:204
  40.6 1.3 pad_maximum_fusion
  42.5 4.4 collective-permute-start.9
  46.9 1.8 convolution_convert_fusion.20.refs_18_
  48.7 1.3 convolution_convert_fusion.9.refs_20_
  51.5 1.9 convolution_convert_fusion.26.refs_4_
  53.5 5.7 %collective-permute-done.1 = bf16[768,1024]{1,0:T(8,128)(2,1)S(1)} collective-permute-done((bf16[768,1024]{1,0:T(8,128)(2,1)S(1)}, bf16[768,1024]{1,0:T(8,128)(2,1)S(1)}, u32[]{:S(2)}, u32[]{:S(2)}) %collective-permute-start.1) | collective-permute-done | bytes 1572896 | tf_op jit(solution)/shard_map/ppermute | solution.py:200
  59.7 7.6 %collective-permute-start.7 = (bf16[512,1024]{1,0:T(8,128)(2,1)S(1)}, bf16[512,1024]{1,0:T(8,128)(2,1)S(1)}, u32[]{:S(2)}, u32[]{:S(2)}) collective-permute-start(bf16[512,1024]{1,0:T(8,128)(2,1)S(1)} %pad_maximum_fusion), channel_id=1, source_target_pairs={{0,8},{8,0},{1,9},{9,1},{2,10},{10,2},{3,11},{11,3},{4,12},{12,4},... | collective-permute-start | bytes 3145736 | tf_op jit(solution)/shard_map/ppermute | solution.py:200
  67.3 1.8 convolution_convert_fusion.3.refs_15_
  69.1 1.3 convolution_convert_fusion.8.refs_22_
  70.4 1.3 convolution_convert_fusion.13.refs_8_
  71.7 1.8 convolution_convert_fusion.5.refs_1_
  74.2 2.1 collective-permute-start.5
  77.1 1.3 convolution_convert_fusion.10.refs_19_
  79.6 10.8 %collective-permute-done.7 = bf16[512,1024]{1,0:T(8,128)(2,1)S(1)} collective-permute-done((bf16[512,1024]{1,0:T(8,128)(2,1)S(1)}, bf16[512,1024]{1,0:T(8,128)(2,1)S(1)}, u32[]{:S(2)}, u32[]{:S(2)}) %collective-permute-start.7) | collective-permute-done | bytes 1048608 | tf_op jit(solution)/shard_map/ppermute | solution.py:200
  92.4 1.6 collective-permute-start.10
  93.9 1.3 convolution_convert_fusion.7.refs_24_
  95.3 2.3 convolution_convert_fusion.1.refs_0_
  97.7 2.4 convolution_convert_fusion.refs_14_
  100.1 2.4 multiply_convert_fusion.query_ref
  108.8 1.8 convolution_convert_fusion.2.refs_17_
  110.6 1.8 convolution_convert_fusion.4.refs_3_
  113.9 1.3 convolution_convert_fusion.6.refs_26_
  116.5 344.2 %attend.1 = bf16[1024,1024]{1,0:T(8,128)(2,1)S(1)} custom-call(s32[8,16]{1,0:T(8,128)S(1)} %fusion.6.table_ref, bf16[1024,1024]{1,0:T(8,128)(2,1)S(1)} %multiply_convert_fusion.query_ref, bf16[1024,1024]{1,0:T(8,128)(2,1)S(1)} %convolution_convert_fusion.1.refs_0_, bf16[768,1024]{1,0:T(8,128)(2,1)S(1)} %convolution_convert_fusion.5.refs_1_, ...), custom_call_target="tpu_custom_call" | custom-call | flops 51539607552 | bytes 31457280 | tf_op jit(solution)/shard_map/attend/pallas_call | solution.py:164
  460.7 3.7 convert_bitcast_fusion
  (48 shorter events, 19.2 us)
Async XLA Ops:
  0.0 460.7 %copy-start = (bf16[1024,1024]{1,0:T(8,128)(2,1)S(1)}, bf16[1024,1024]{1,0:T(8,128)(2,1)}, u32[]{:S(2)}) copy-start(bf16[1024,1024]{1,0:T(8,128)(2,1)} %param.6) | copy-start | bytes 6291460
  1.2 12.9 %collective-permute-start = (bf16[256,1024]{1,0:T(8,128)(2,1)S(1)}, bf16[256,1024]{1,0:T(8,128)(2,1)S(1)}, u32[]{:S(2)}, u32[]{:S(2)}) collective-permute-start(bf16[256,1024]{1,0:T(8,128)(2,1)S(1)} %slice_bitcast_fusion), channel_id=1, source_target_pairs={{0,8},{8,0},{1,9},{9,1},{2,10},{10,2},{3,11},{11,3},{4,12},{12,4},... | collective-permute-start | bytes 1572872 | tf_op jit(solution)/shard_map/ppermute | solution.py:200
  14.1 9.7 %copy-start.2 = (s32[16,16]{1,0:T(8,128)S(1)}, s32[16,16]{1,0:T(8,128)}, u32[]{:S(2)}) copy-start(s32[16,16]{1,0:T(8,128)} %param.7) | copy-start | bytes 3076
  15.2 12.0 %collective-permute-start.3 = (bf16[256,1024]{1,0:T(8,128)(2,1)S(1)}, bf16[256,1024]{1,0:T(8,128)(2,1)}, u32[]{:S(2)}, u32[]{:S(2)}) collective-permute-start(bf16[256,1024]{1,0:T(8,128)(2,1)S(1)} %slice_select_fusion), channel_id=1, source_target_pairs={{0,6},{1,7},{2,0},{3,1},{4,2},{5,3},{6,4},{7,5},{8,14},{9,15},{10,... | collective-permute-start | bytes 1572872 | tf_op jit(solution)/shard_map/ppermute | solution.py:204
  15.4 25.2 %collective-permute-start.2 = (bf16[256,1024]{1,0:T(8,128)(2,1)S(1)}, bf16[256,1024]{1,0:T(8,128)(2,1)}, u32[]{:S(2)}, u32[]{:S(2)}) collective-permute-start(bf16[256,1024]{1,0:T(8,128)(2,1)S(1)} %slice_select_fusion), channel_id=1, source_target_pairs={{0,2},{1,3},{2,4},{3,5},{4,6},{5,7},{6,0},{7,1},{8,10},{9,11},{10,... | collective-permute-start | bytes 1572872 | tf_op jit(solution)/shard_map/ppermute | solution.py:204
  16.7 30.2 %collective-permute-start.6 = (bf16[256,1024]{1,0:T(8,128)(2,1)S(1)}, bf16[256,1024]{1,0:T(8,128)(2,1)}, u32[]{:S(2)}, u32[]{:S(2)}) collective-permute-start(bf16[256,1024]{1,0:T(8,128)(2,1)S(1)} %collective-permute-done), channel_id=1, source_target_pairs={{0,1},{9,8},{1,2},{10,9},{2,3},{11,10},{3,4},{12,11},{4,5},{13,12}... | collective-permute-start | bytes 1572872 | tf_op jit(solution)/shard_map/ppermute | solution.py:209
  21.9 24.9 %copy-start.4 = (bf16[1024,1024]{1,0:T(8,128)(2,1)S(1)}, bf16[1024,1024]{1,0:T(8,128)(2,1)}, u32[]{:S(2)}) copy-start(bf16[1024,1024]{1,0:T(8,128)(2,1)} %get-tuple-element.38) | copy-start | bytes 6291460
  23.6 35.5 %collective-permute-start.1 = (bf16[768,1024]{1,0:T(8,128)(2,1)S(1)}, bf16[768,1024]{1,0:T(8,128)(2,1)S(1)}, u32[]{:S(2)}, u32[]{:S(2)}) collective-permute-start(bf16[768,1024]{1,0:T(8,128)(2,1)S(1)} %slice.20), channel_id=1, source_target_pairs={{0,8},{8,0},{1,9},{9,1},{2,10},{10,2},{3,11},{11,3},{4,12},{12,4},... | collective-permute-start | bytes 4718600 | tf_op jit(solution)/shard_map/ppermute | solution.py:200
  41.9 37.8 %collective-permute-start.8 = (bf16[256,1024]{1,0:T(8,128)(2,1)S(1)}, bf16[256,1024]{1,0:T(8,128)(2,1)S(1)}, u32[]{:S(2)}, u32[]{:S(2)}) collective-permute-start(bf16[256,1024]{1,0:T(8,128)(2,1)S(1)} %slice_select_fusion), channel_id=1, source_target_pairs={{0,4},{1,5},{2,6},{3,7},{4,0},{5,1},{6,2},{7,3},{8,12},{9,13},{10,... | collective-permute-start | bytes 1572872 | tf_op jit(solution)/shard_map/ppermute | solution.py:204
  42.5 26.6 %collective-permute-start.9 = (bf16[512,1024]{1,0:T(8,128)(2,1)S(1)}, bf16[512,1024]{1,0:T(8,128)(2,1)S(1)}, u32[]{:S(2)}, u32[]{:S(2)}) collective-permute-start(bf16[512,1024]{1,0:T(8,128)(2,1)S(1)} %pad_maximum_fusion), channel_id=1, source_target_pairs={{0,1},{1,0},{2,3},{3,2},{4,5},{5,4},{6,7},{7,6},{8,9},{9,8},{10,11... | collective-permute-start | bytes 3145736 | tf_op jit(solution)/shard_map/ppermute | solution.py:201
  48.7 1.6 copy-start.3
  51.5 7.6 %copy-start.1 = (bf16[1,1024,1024]{2,1,0:T(8,128)(2,1)S(1)}, bf16[1,1024,1024]{2,1,0:T(8,128)(2,1)}, u32[]{:S(2)}) copy-start(bf16[1,1024,1024]{2,1,0:T(8,128)(2,1)} %param.4) | copy-start | bytes 6291460
  59.6 17.5 %collective-permute-start.4 = (bf16[512,1024]{1,0:T(8,128)(2,1)S(1)}, bf16[512,1024]{1,0:T(8,128)(2,1)S(1)}, u32[]{:S(2)}, u32[]{:S(2)}) collective-permute-start(bf16[512,1024]{1,0:T(8,128)(2,1)S(1)} %maximum_select_fusion), channel_id=1, source_target_pairs={{0,1},{1,0},{2,3},{3,2},{4,5},{5,4},{6,7},{7,6},{8,9},{9,8},{10,11... | collective-permute-start | bytes 3145736 | tf_op jit(solution)/shard_map/ppermute | solution.py:201
  59.7 30.7 %collective-permute-start.7 = (bf16[512,1024]{1,0:T(8,128)(2,1)S(1)}, bf16[512,1024]{1,0:T(8,128)(2,1)S(1)}, u32[]{:S(2)}, u32[]{:S(2)}) collective-permute-start(bf16[512,1024]{1,0:T(8,128)(2,1)S(1)} %pad_maximum_fusion), channel_id=1, source_target_pairs={{0,8},{8,0},{1,9},{9,1},{2,10},{10,2},{3,11},{11,3},{4,12},{12,4},... | collective-permute-start | bytes 3145736 | tf_op jit(solution)/shard_map/ppermute | solution.py:200
  74.2 34.5 %collective-permute-start.5 = (bf16[768,1024]{1,0:T(8,128)(2,1)S(1)}, bf16[768,1024]{1,0:T(8,128)(2,1)S(1)}, u32[]{:S(2)}, u32[]{:S(2)}) collective-permute-start(bf16[768,1024]{1,0:T(8,128)(2,1)S(1)} %collective-permute-done.1), channel_id=1, source_target_pairs={{0,1},{9,8},{1,2},{10,9},{2,3},{11,10},{3,4},{12,11},{4,5},{13,12}... | collective-permute-start | bytes 4718600 | tf_op jit(solution)/shard_map/ppermute | solution.py:209
  91.2 13.3 %collective-permute-start.11 = (bf16[256,1024]{1,0:T(8,128)(2,1)S(1)}, bf16[256,1024]{1,0:T(8,128)(2,1)S(1)}, u32[]{:S(2)}, u32[]{:S(2)}) collective-permute-start(bf16[256,1024]{1,0:T(8,128)(2,1)S(1)} %collective-permute-done.8), channel_id=1, source_target_pairs={{0,8},{8,0},{1,9},{9,1},{2,10},{10,2},{3,11},{11,3},{4,12},{12,4},... | collective-permute-start | bytes 1572872 | tf_op jit(solution)/shard_map/ppermute | solution.py:200
  92.4 14.9 %collective-permute-start.10 = (bf16[256,1024]{1,0:T(8,128)(2,1)S(1)}, bf16[256,1024]{1,0:T(8,128)(2,1)S(1)}, u32[]{:S(2)}, u32[]{:S(2)}) collective-permute-start(bf16[256,1024]{1,0:T(8,128)(2,1)S(1)} %collective-permute-done.8), channel_id=1, source_target_pairs={{0,1},{1,0},{2,3},{3,2},{4,5},{5,4},{6,7},{7,6},{8,9},{9,8},{10,11... | collective-permute-start | bytes 1572872 | tf_op jit(solution)/shard_map/ppermute | solution.py:201
  95.2 18.7 %collective-permute-start.12 = (bf16[512,1024]{1,0:T(8,128)(2,1)S(1)}, bf16[512,1024]{1,0:T(8,128)(2,1)S(1)}, u32[]{:S(2)}, u32[]{:S(2)}) collective-permute-start(bf16[512,1024]{1,0:T(8,128)(2,1)S(1)} %collective-permute-done.7), channel_id=1, source_target_pairs={{0,1},{1,0},{2,3},{3,2},{4,5},{5,4},{6,7},{7,6},{8,9},{9,8},{10,11... | collective-permute-start | bytes 3145736 | tf_op jit(solution)/shard_map/ppermute | solution.py:201
  97.7 2.4 copy-start.5
  104.5 8.0 %collective-permute-start.13 = (bf16[256,1024]{1,0:T(8,128)(2,1)S(1)}, bf16[256,1024]{1,0:T(8,128)(2,1)S(1)}, u32[]{:S(2)}, u32[]{:S(2)}) collective-permute-start(bf16[256,1024]{1,0:T(8,128)(2,1)S(1)} %collective-permute-done.11), channel_id=1, source_target_pairs={{0,1},{1,0},{2,3},{3,2},{4,5},{5,4},{6,7},{7,6},{8,9},{9,8},{10,11... | collective-permute-start | bytes 1572872 | tf_op jit(solution)/shard_map/ppermute | solution.py:201

commit v4 on v3

--- a/solution.py
+++ b/solution.py
@@ -289,7 +289,7 @@
     _, key_weight, value_weight = weights
     keys = [project_rows(rows, key_weight) for rows in pieces]
     values = [project_columns(value_weight, rows) for rows in pieces]
-    mixed = attend(table, query, keys, values, 4, 2)
+    mixed = attend(table, query, keys, values, 4, 4)
     out = jnp.dot(mixed, out_weight, preferred_element_type=jnp.float32).astype(jnp.bfloat16)
     return out.reshape(tokens.shape)
 

time: 465 us -> 469 us (level); the launches traced: 464 us -> 461 us
  transfers between devices with their start and end apart: 14 -> 14, of which waited for: 5 -> 5; matrix products, arithmetic and copies ran while one was open for 8% -> 9% of each run, Pallas kernels for 2% -> 2%
where the time goes in v4:
time: 469 us; the launch traced here: 461 us
  Pallas kernels  349 us (74%)
  matrix products  42 us (9%)
  waiting for transfers between devices  36.2 us (8%)
  starting transfers between devices  26.9 us (6%)
    pallas_call x1, Pallas kernels, attend(): pl.pallas_call(functools.partial(attend_kernel, blocks, count, chunk, tog...  341 us
    dot_general x15, matrix products, project_columns(): lax.dot_general(weight, rows, (((1,), (1,)), ((), ())), preferred_element...  20.6 us
    ppermute x4, waiting for transfers between devices, rows_by_axes(): swap = lambda rows: lax.ppermute(rows, 'head', [(0, 1), (1, 0)])  19.4 us
    dot_general x14, matrix products, project_rows(): jnp.dot(rows, weight, preferred_element_type=jnp.float32)  17.8 us
    ppermute x3, waiting for transfers between devices, along(): lax.ppermute(rows, 'blk', [(s, (s + 2 * k) % strides) for s in range(stri...  16.8 us
    ppermute x4, starting transfers between devices, rows_by_axes(): swap = lambda rows: lax.ppermute(rows, 'head', [(0, 1), (1, 0)])  10.2 us
  transfers between devices with their start and end apart: 14, of which 5 were waited for; matrix products, arithmetic and copies ran while one was open for 9% of the time, Pallas kernels for 2%

profile of v4, /device:TPU:11, one launch (start us, length us, event | category | flops | bytes accessed | tf_op | source)
XLA Modules:
  0.0 461.3 jit_solution(13068909364574708819)
XLA Ops:
  1.2 1.3 collective-permute-start
  2.5 8.6 %split_weights.1 = (bf16[1024,1024]{1,0:T(8,128)(2,1)}, bf16[1024,1024]{1,0:T(8,128)(2,1)}, bf16[1024,1024]{1,0:T(8,128)(2,1)}) custom-call(bf16[1024,3072]{1,0:T(8,128)(2,1)} %weight_ref.1), custom_call_target="tpu_custom_call" | custom-call | bytes 12582912 | tf_op jit(solution)/shard_map/split_weights/pallas_call | solution.py:41
  11.1 3.0 collective-permute-done
  15.4 1.3 collective-permute-start.2
  16.7 5.2 %collective-permute-start.6 = (bf16[256,1024]{1,0:T(8,128)(2,1)S(1)}, bf16[256,1024]{1,0:T(8,128)(2,1)}, u32[]{:S(2)}, u32[]{:S(2)}) collective-permute-start(bf16[256,1024]{1,0:T(8,128)(2,1)S(1)} %collective-permute-done), channel_id=1, source_target_pairs={{0,1},{9,8},{1,2},{10,9},{2,3},{11,10},{3,4},{12,11},{4,5},{13,12}... | collective-permute-start | bytes 1572872 | tf_op jit(solution)/shard_map/ppermute | solution.py:209
  22.0 1.7 slice.20
  23.8 3.4 collective-permute-done.3
  27.2 13.3 %collective-permute-done.2 = bf16[256,1024]{1,0:T(8,128)(2,1)} collective-permute-done((bf16[256,1024]{1,0:T(8,128)(2,1)S(1)}, bf16[256,1024]{1,0:T(8,128)(2,1)}, u32[]{:S(2)}, u32[]{:S(2)}) %collective-permute-start.2) | collective-permute-done | bytes 524320 | tf_op jit(solution)/shard_map/ppermute | solution.py:204
  40.6 1.3 pad_maximum_fusion
  42.5 4.4 collective-permute-start.9
  46.9 1.8 convolution_convert_fusion.20.refs_18_
  48.7 1.3 convolution_convert_fusion.9.refs_20_
  51.5 1.9 convolution_convert_fusion.26.refs_4_
  53.5 5.7 %collective-permute-done.1 = bf16[768,1024]{1,0:T(8,128)(2,1)S(1)} collective-permute-done((bf16[768,1024]{1,0:T(8,128)(2,1)S(1)}, bf16[768,1024]{1,0:T(8,128)(2,1)S(1)}, u32[]{:S(2)}, u32[]{:S(2)}) %collective-permute-start.1) | collective-permute-done | bytes 1572896 | tf_op jit(solution)/shard_map/ppermute | solution.py:200
  59.7 7.6 %collective-permute-start.7 = (bf16[512,1024]{1,0:T(8,128)(2,1)S(1)}, bf16[512,1024]{1,0:T(8,128)(2,1)S(1)}, u32[]{:S(2)}, u32[]{:S(2)}) collective-permute-start(bf16[512,1024]{1,0:T(8,128)(2,1)S(1)} %pad_maximum_fusion), channel_id=1, source_target_pairs={{0,8},{8,0},{1,9},{9,1},{2,10},{10,2},{3,11},{11,3},{4,12},{12,4},... | collective-permute-start | bytes 3145736 | tf_op jit(solution)/shard_map/ppermute | solution.py:200
  67.3 1.8 convolution_convert_fusion.3.refs_15_
  69.1 1.3 convolution_convert_fusion.8.refs_22_
  71.7 1.8 convolution_convert_fusion.5.refs_1_
  74.2 2.1 collective-permute-start.5
  77.1 1.3 convolution_convert_fusion.10.refs_19_
  79.6 10.8 %collective-permute-done.7 = bf16[512,1024]{1,0:T(8,128)(2,1)S(1)} collective-permute-done((bf16[512,1024]{1,0:T(8,128)(2,1)S(1)}, bf16[512,1024]{1,0:T(8,128)(2,1)S(1)}, u32[]{:S(2)}, u32[]{:S(2)}) %collective-permute-start.7) | collective-permute-done | bytes 1048608 | tf_op jit(solution)/shard_map/ppermute | solution.py:200
  92.4 1.6 collective-permute-start.10
  93.9 1.3 convolution_convert_fusion.7.refs_24_
  95.3 2.3 convolution_convert_fusion.1.refs_0_
  97.7 2.4 convolution_convert_fusion.refs_14_
  100.1 2.4 multiply_convert_fusion.query_ref
  103.2 1.3 convolution_convert_fusion.12.refs_10_
  108.8 1.8 convolution_convert_fusion.2.refs_17_
  110.6 1.8 convolution_convert_fusion.4.refs_3_
  113.9 1.3 convolution_convert_fusion.6.refs_26_
  116.5 340.6 %attend.1 = bf16[1024,1024]{1,0:T(8,128)(2,1)S(1)} custom-call(s32[8,16]{1,0:T(8,128)S(1)} %fusion.6.table_ref, bf16[1024,1024]{1,0:T(8,128)(2,1)S(1)} %multiply_convert_fusion.query_ref, bf16[1024,1024]{1,0:T(8,128)(2,1)S(1)} %convolution_convert_fusion.1.refs_0_, bf16[768,1024]{1,0:T(8,128)(2,1)S(1)} %convolution_convert_fusion.5.refs_1_, ...), custom_call_target="tpu_custom_call" | custom-call | flops 51539607552 | bytes 31457280 | tf_op jit(solution)/shard_map/attend/pallas_call | solution.py:164
  457.2 3.7 convert_bitcast_fusion
  (48 shorter events, 19.2 us)
Async XLA Ops:
  0.0 457.1 %copy-start = (bf16[1024,1024]{1,0:T(8,128)(2,1)S(1)}, bf16[1024,1024]{1,0:T(8,128)(2,1)}, u32[]{:S(2)}) copy-start(bf16[1024,1024]{1,0:T(8,128)(2,1)} %param.6) | copy-start | bytes 6291460
  1.2 12.9 %collective-permute-start = (bf16[256,1024]{1,0:T(8,128)(2,1)S(1)}, bf16[256,1024]{1,0:T(8,128)(2,1)S(1)}, u32[]{:S(2)}, u32[]{:S(2)}) collective-permute-start(bf16[256,1024]{1,0:T(8,128)(2,1)S(1)} %slice_bitcast_fusion), channel_id=1, source_target_pairs={{0,8},{8,0},{1,9},{9,1},{2,10},{10,2},{3,11},{11,3},{4,12},{12,4},... | collective-permute-start | bytes 1572872 | tf_op jit(solution)/shard_map/ppermute | solution.py:200
  14.1 9.7 %copy-start.2 = (s32[16,16]{1,0:T(8,128)S(1)}, s32[16,16]{1,0:T(8,128)}, u32[]{:S(2)}) copy-start(s32[16,16]{1,0:T(8,128)} %param.7) | copy-start | bytes 3076
  15.2 12.0 %collective-permute-start.3 = (bf16[256,1024]{1,0:T(8,128)(2,1)S(1)}, bf16[256,1024]{1,0:T(8,128)(2,1)}, u32[]{:S(2)}, u32[]{:S(2)}) collective-permute-start(bf16[256,1024]{1,0:T(8,128)(2,1)S(1)} %slice_select_fusion), channel_id=1, source_target_pairs={{0,6},{1,7},{2,0},{3,1},{4,2},{5,3},{6,4},{7,5},{8,14},{9,15},{10,... | collective-permute-start | bytes 1572872 | tf_op jit(solution)/shard_map/ppermute | solution.py:204
  15.4 25.2 %collective-permute-start.2 = (bf16[256,1024]{1,0:T(8,128)(2,1)S(1)}, bf16[256,1024]{1,0:T(8,128)(2,1)}, u32[]{:S(2)}, u32[]{:S(2)}) collective-permute-start(bf16[256,1024]{1,0:T(8,128)(2,1)S(1)} %slice_select_fusion), channel_id=1, source_target_pairs={{0,2},{1,3},{2,4},{3,5},{4,6},{5,7},{6,0},{7,1},{8,10},{9,11},{10,... | collective-permute-start | bytes 1572872 | tf_op jit(solution)/shard_map/ppermute | solution.py:204
  16.7 30.2 %collective-permute-start.6 = (bf16[256,1024]{1,0:T(8,128)(2,1)S(1)}, bf16[256,1024]{1,0:T(8,128)(2,1)}, u32[]{:S(2)}, u32[]{:S(2)}) collective-permute-start(bf16[256,1024]{1,0:T(8,128)(2,1)S(1)} %collective-permute-done), channel_id=1, source_target_pairs={{0,1},{9,8},{1,2},{10,9},{2,3},{11,10},{3,4},{12,11},{4,5},{13,12}... | collective-permute-start | bytes 1572872 | tf_op jit(solution)/shard_map/ppermute | solution.py:209
  21.9 24.9 %copy-start.4 = (bf16[1024,1024]{1,0:T(8,128)(2,1)S(1)}, bf16[1024,1024]{1,0:T(8,128)(2,1)}, u32[]{:S(2)}) copy-start(bf16[1024,1024]{1,0:T(8,128)(2,1)} %get-tuple-element.38) | copy-start | bytes 6291460
  23.6 35.5 %collective-permute-start.1 = (bf16[768,1024]{1,0:T(8,128)(2,1)S(1)}, bf16[768,1024]{1,0:T(8,128)(2,1)S(1)}, u32[]{:S(2)}, u32[]{:S(2)}) collective-permute-start(bf16[768,1024]{1,0:T(8,128)(2,1)S(1)} %slice.20), channel_id=1, source_target_pairs={{0,8},{8,0},{1,9},{9,1},{2,10},{10,2},{3,11},{11,3},{4,12},{12,4},... | collective-permute-start | bytes 4718600 | tf_op jit(solution)/shard_map/ppermute | solution.py:200
  41.9 37.8 %collective-permute-start.8 = (bf16[256,1024]{1,0:T(8,128)(2,1)S(1)}, bf16[256,1024]{1,0:T(8,128)(2,1)S(1)}, u32[]{:S(2)}, u32[]{:S(2)}) collective-permute-start(bf16[256,1024]{1,0:T(8,128)(2,1)S(1)} %slice_select_fusion), channel_id=1, source_target_pairs={{0,4},{1,5},{2,6},{3,7},{4,0},{5,1},{6,2},{7,3},{8,12},{9,13},{10,... | collective-permute-start | bytes 1572872 | tf_op jit(solution)/shard_map/ppermute | solution.py:204
  42.5 26.6 %collective-permute-start.9 = (bf16[512,1024]{1,0:T(8,128)(2,1)S(1)}, bf16[512,1024]{1,0:T(8,128)(2,1)S(1)}, u32[]{:S(2)}, u32[]{:S(2)}) collective-permute-start(bf16[512,1024]{1,0:T(8,128)(2,1)S(1)} %pad_maximum_fusion), channel_id=1, source_target_pairs={{0,1},{1,0},{2,3},{3,2},{4,5},{5,4},{6,7},{7,6},{8,9},{9,8},{10,11... | collective-permute-start | bytes 3145736 | tf_op jit(solution)/shard_map/ppermute | solution.py:201
  48.7 1.6 copy-start.3
  51.5 7.6 %copy-start.1 = (bf16[1,1024,1024]{2,1,0:T(8,128)(2,1)S(1)}, bf16[1,1024,1024]{2,1,0:T(8,128)(2,1)}, u32[]{:S(2)}) copy-start(bf16[1,1024,1024]{2,1,0:T(8,128)(2,1)} %param.4) | copy-start | bytes 6291460
  59.6 17.5 %collective-permute-start.4 = (bf16[512,1024]{1,0:T(8,128)(2,1)S(1)}, bf16[512,1024]{1,0:T(8,128)(2,1)S(1)}, u32[]{:S(2)}, u32[]{:S(2)}) collective-permute-start(bf16[512,1024]{1,0:T(8,128)(2,1)S(1)} %maximum_select_fusion), channel_id=1, source_target_pairs={{0,1},{1,0},{2,3},{3,2},{4,5},{5,4},{6,7},{7,6},{8,9},{9,8},{10,11... | collective-permute-start | bytes 3145736 | tf_op jit(solution)/shard_map/ppermute | solution.py:201
  59.7 30.8 %collective-permute-start.7 = (bf16[512,1024]{1,0:T(8,128)(2,1)S(1)}, bf16[512,1024]{1,0:T(8,128)(2,1)S(1)}, u32[]{:S(2)}, u32[]{:S(2)}) collective-permute-start(bf16[512,1024]{1,0:T(8,128)(2,1)S(1)} %pad_maximum_fusion), channel_id=1, source_target_pairs={{0,8},{8,0},{1,9},{9,1},{2,10},{10,2},{3,11},{11,3},{4,12},{12,4},... | collective-permute-start | bytes 3145736 | tf_op jit(solution)/shard_map/ppermute | solution.py:200
  74.2 34.5 %collective-permute-start.5 = (bf16[768,1024]{1,0:T(8,128)(2,1)S(1)}, bf16[768,1024]{1,0:T(8,128)(2,1)S(1)}, u32[]{:S(2)}, u32[]{:S(2)}) collective-permute-start(bf16[768,1024]{1,0:T(8,128)(2,1)S(1)} %collective-permute-done.1), channel_id=1, source_target_pairs={{0,1},{9,8},{1,2},{10,9},{2,3},{11,10},{3,4},{12,11},{4,5},{13,12}... | collective-permute-start | bytes 4718600 | tf_op jit(solution)/shard_map/ppermute | solution.py:209
  91.2 13.3 %collective-permute-start.11 = (bf16[256,1024]{1,0:T(8,128)(2,1)S(1)}, bf16[256,1024]{1,0:T(8,128)(2,1)S(1)}, u32[]{:S(2)}, u32[]{:S(2)}) collective-permute-start(bf16[256,1024]{1,0:T(8,128)(2,1)S(1)} %collective-permute-done.8), channel_id=1, source_target_pairs={{0,8},{8,0},{1,9},{9,1},{2,10},{10,2},{3,11},{11,3},{4,12},{12,4},... | collective-permute-start | bytes 1572872 | tf_op jit(solution)/shard_map/ppermute | solution.py:200
  92.4 14.9 %collective-permute-start.10 = (bf16[256,1024]{1,0:T(8,128)(2,1)S(1)}, bf16[256,1024]{1,0:T(8,128)(2,1)S(1)}, u32[]{:S(2)}, u32[]{:S(2)}) collective-permute-start(bf16[256,1024]{1,0:T(8,128)(2,1)S(1)} %collective-permute-done.8), channel_id=1, source_target_pairs={{0,1},{1,0},{2,3},{3,2},{4,5},{5,4},{6,7},{7,6},{8,9},{9,8},{10,11... | collective-permute-start | bytes 1572872 | tf_op jit(solution)/shard_map/ppermute | solution.py:201
  95.2 18.7 %collective-permute-start.12 = (bf16[512,1024]{1,0:T(8,128)(2,1)S(1)}, bf16[512,1024]{1,0:T(8,128)(2,1)S(1)}, u32[]{:S(2)}, u32[]{:S(2)}) collective-permute-start(bf16[512,1024]{1,0:T(8,128)(2,1)S(1)} %collective-permute-done.7), channel_id=1, source_target_pairs={{0,1},{1,0},{2,3},{3,2},{4,5},{5,4},{6,7},{7,6},{8,9},{9,8},{10,11... | collective-permute-start | bytes 3145736 | tf_op jit(solution)/shard_map/ppermute | solution.py:201
  97.7 2.4 copy-start.5
  104.5 8.0 %collective-permute-start.13 = (bf16[256,1024]{1,0:T(8,128)(2,1)S(1)}, bf16[256,1024]{1,0:T(8,128)(2,1)S(1)}, u32[]{:S(2)}, u32[]{:S(2)}) collective-permute-start(bf16[256,1024]{1,0:T(8,128)(2,1)S(1)} %collective-permute-done.11), channel_id=1, source_target_pairs={{0,1},{1,0},{2,3},{3,2},{4,5},{5,4},{6,7},{7,6},{8,9},{9,8},{10,11... | collective-permute-start | bytes 1572872 | tf_op jit(solution)/shard_map/ppermute | solution.py:201
